TPU v7x, 512 devices: a whole 4x8x8 slice. The times are simulated.
512 devices in a mesh: tensor: 16 (over y_hi, z), shard: 16 (over x, y_lo), replica: 2 (over core).
Axes of the slice: x: 4, y: 8 (y_hi: 2, y_lo: 4; y = y_hi * 4 + y_lo), z: 8, core: 2. Of those that a mesh axis runs over, the one named last changes fastest.
Arguments:
- tokens: bfloat16 [4096, 4096], P(('tensor', 'shard', 'replica')), may hold values from -110 to 110
- grad_out: bfloat16 [4096, 4096], P(('tensor', 'shard', 'replica')), may hold values from -6 to 6
- norm_gain: float32 [4096], replicated, may hold values from 0.1 to 1.9
- norm_bias: float32 [4096], replicated, may hold values from -3 to 3
- up_weight: bfloat16 [4096, 8192], P('shard', 'tensor'), may hold values from -0.09375 to 0.09375
- up_bias: float32 [8192], P('tensor'), may hold values from -3 to 3
- down_weight: bfloat16 [8192, 4096], P('tensor', 'shard'), may hold values from -0.0625 to 0.0625
Outputs:
- input_grad: bfloat16 [4096, 4096], P(('tensor', 'shard', 'replica'))
- up_grad: float32 [4096, 8192], P(('shard', 'replica'), 'tensor')
- down_grad: float32 [8192, 4096], P('tensor', ('shard', 'replica'))
- up_bias_grad: float32 [8192], P('tensor')
- gain_grad: float32 [4096], replicated
- bias_grad: float32 [4096], replicated
All inputs are finite; a program needn't handle non-finite values.
Results may differ from a plain program's by a relative error of at most 0.007.
Values may be sent and summed in bfloat16 or wider, within the bound.
A program may use at most 64 MiB of HBM per device.

v0:
```python
import jax
import jax.numpy as jnp
from jax import lax
from jax.sharding import PartitionSpec as P


def dot_nt(left, right):
    return lax.dot_general(
        left, right, (((1,), (1,)), ((), ())), preferred_element_type=jnp.float32
    )


def dot_tn(left, right):
    return lax.dot_general(
        left, right, (((0,), (0,)), ((), ())), preferred_element_type=jnp.float32
    )


def normalize(values):
    widened = values.astype(jnp.float32)
    centred = widened - jnp.mean(widened, axis=-1, keepdims=True)
    variance = jnp.mean(centred * centred, axis=-1, keepdims=True)
    inverse_std = lax.rsqrt(variance + 1e-05)
    return (centred * inverse_std, inverse_std)


def norm_back(d_normed, standard, inverse_std, gain):
    scaled = d_normed * gain
    first = jnp.mean(scaled, axis=-1, keepdims=True)
    second = jnp.mean(scaled * standard, axis=-1, keepdims=True)
    return inverse_std * (scaled - first - standard * second)


def gelu_back(pre_act, upstream):
    result, pull_back = jax.vjp(jax.nn.gelu, pre_act)
    return pull_back(upstream)[0]


def shards(tokens, grad_out, norm_gain, norm_bias, up_weight, up_bias, down_weight):
    standard, inverse_std = normalize(tokens)
    normed_local = (standard * norm_gain + norm_bias).astype(jnp.bfloat16)
    normed, grads_all = (
        lax.all_gather(normed_local, "tensor", axis=0, tiled=True),
        lax.all_gather(grad_out, "tensor", axis=0, tiled=True),
    )
    up_full = lax.all_gather(up_weight, "shard", axis=0, tiled=True)
    d_act = dot_nt(grads_all, lax.all_gather(down_weight, "shard", axis=1, tiled=True))
    pre_act = jnp.dot(normed, up_full, preferred_element_type=jnp.float32) + up_bias
    act = jax.nn.gelu(pre_act).astype(jnp.bfloat16)
    d_hidden = gelu_back(pre_act, d_act).astype(jnp.bfloat16)
    hidden_part = jnp.sum(d_hidden.astype(jnp.float32), axis=0)
    d_normed = lax.psum_scatter(
        dot_nt(d_hidden, up_full), "tensor", scatter_dimension=0, tiled=True
    )
    gain_grad, bias_grad = lax.psum(
        (jnp.sum(d_normed * standard, axis=0), jnp.sum(d_normed, axis=0)),
        ("tensor", "shard", "replica"),
    )
    up_bias_grad = lax.psum(hidden_part, ("shard", "replica"))
    d_in = norm_back(d_normed, standard, inverse_std, norm_gain)
    input_grad = (grad_out.astype(jnp.float32) + d_in).astype(jnp.bfloat16)
    normed_cols, grad_cols = (
        lax.all_to_all(normed, "shard", split_axis=1, concat_axis=0, tiled=True),
        lax.all_to_all(grads_all, "shard", split_axis=1, concat_axis=0, tiled=True),
    )
    act_piece = lax.all_gather(act, "shard", axis=0, tiled=True)
    hidden_piece = lax.all_gather(d_hidden, "shard", axis=0, tiled=True)
    up_part = dot_tn(normed_cols, hidden_piece)
    down_part = dot_tn(act_piece, grad_cols)
    up_grad, down_grad = (
        lax.psum_scatter(up_part, "replica", scatter_dimension=0, tiled=True),
        lax.psum_scatter(down_part, "replica", scatter_dimension=1, tiled=True),
    )
    return (input_grad, up_grad, down_grad, up_bias_grad, gain_grad, bias_grad)


def solution(mesh):
    return jax.shard_map(
        shards,
        mesh=mesh,
        in_specs=(
            P(("tensor", "shard", "replica"), None),
            P(("tensor", "shard", "replica"), None),
            P(),
            P(),
            P("shard", "tensor"),
            P("tensor"),
            P("tensor", "shard"),
        ),
        out_specs=(
            P(("tensor", "shard", "replica"), None),
            P(("shard", "replica"), "tensor"),
            P("tensor", ("shard", "replica")),
            P("tensor"),
            P(),
            P(),
        ),
        check_vma=False,
    )
```

profile of v0, /device:TPU:1, one launch (start us, length us, event | category | flops | bytes accessed | tf_op | source)
XLA Modules:
  0.0 942.2 jit_solution(6335368522828959445)
XLA Ops:
  7.2 0.0 copy-start.5
  7.2 0.0 all-gather.7.cloned.1.call-start
  7.2 0.7 all-gather.7.cloned.1.call-update
  7.9 0.0 all-gather.9.cloned.1.call-start
  8.0 0.7 all-gather.9.cloned.1.call-update
  8.7 0.0 all-gather.11.cloned.1.call-start
  8.7 1.0 convert_reduce_fusion.1
  9.7 1.1 fusion.21
  10.8 1.6 fusion.14
  12.4 0.0 all-gather.11.cloned.1.call-update
  12.4 0.0 all-gather.13.cloned.1.call-start
  12.4 0.5 all-gather.13.cloned.1.call-update
  13.0 0.0 all-gather.15.cloned.1.call-start
  13.0 88.9 %all-gather.7.cloned.1.call-done = bf16[128,4096]{1,0:T(8,128)(2,1)} async-done(((bf16[8,4096]{1,0:T(8,128)(2,1)}), bf16[128,4096]{1,0:T(8,128)(2,1)}) %all-gather.7.cloned.1.call-update) | async-done | bytes 1048592 | tf_op jit(solution)/shard_map/all_gather | solution.py:44
  101.9 113.1 %all-gather.9.cloned.1.call-done = bf16[512,4096]{1,0:T(8,128)(2,1)} async-done(((bf16[512,256]{1,0:T(8,128)(2,1)}), bf16[512,4096]{1,0:T(8,128)(2,1)}) %all-gather.9.cloned.1.call-update) | async-done | bytes 4194320 | tf_op jit(solution)/shard_map/all_gather | solution.py:47
  215.0 4.0 fusion.23
  219.1 86.5 %all-gather.11.cloned.1.call-done = bf16[128,4096]{1,0:T(8,128)(2,1)} async-done(((bf16[8,4096]{1,0:T(8,128)(2,1)}), bf16[128,4096]{1,0:T(8,128)(2,1)}) %all-gather.11.cloned.1.call-update) | async-done | bytes 1048592 | tf_op jit(solution)/shard_map/all_gather | solution.py:43
  305.6 107.0 %all-gather.13.cloned.1.call-done = bf16[4096,512]{1,0:T(8,128)(2,1)} async-done(((bf16[256,512]{1,0:T(8,128)(2,1)}), bf16[4096,512]{1,0:T(8,128)(2,1)}) %all-gather.13.cloned.1.call-update) | async-done | bytes 4194320 | tf_op jit(solution)/shard_map/all_gather | solution.py:46
  412.6 0.0 copy-done.5
  412.6 4.1 convert_reduce_fusion
  416.7 0.0 all-gather.15.cloned.1.call-update
  416.7 0.0 all-gather.17.cloned.1.call-start
  416.8 0.5 all-gather.17.cloned.1.call-update
  417.3 0.0 copy-start.2
  417.3 0.0 reduce-scatter.4.cloned.1.call-start
  417.3 5.2 fusion.24
  422.5 0.0 copy-start
  422.5 0.0 reduce-scatter.4.cloned.1.call-update
  422.5 0.0 copy-done.2
  422.5 1.1 copy.22
  423.7 3.7 all-to-all-start
  427.3 0.0 copy-done
  427.3 1.3 copy.18
  428.6 46.8 %all-to-all-done = bf16[128,16,256]{2,0,1:T(8,128)(2,1)S(1)} async-done(((bf16[128,16,256]{2,0,1:T(8,128)(2,1)}), bf16[128,16,256]{2,0,1:T(8,128)(2,1)S(1)}, u32[]{:S(2)}, u32[]{:S(2)}) %all-to-all-start) | async-done | bytes 1048608 | tf_op jit(solution)/shard_map/all_to_all | solution.py:63
  475.5 4.5 all-to-all-start.1
  479.9 0.0 reduce-scatter.6.cloned.1.call-start
  480.0 33.9 %all-gather.15.cloned.1.call-done = bf16[2048,512]{1,0:T(8,128)(2,1)} async-done(((bf16[128,512]{1,0:T(8,128)(2,1)}), bf16[2048,512]{1,0:T(8,128)(2,1)}) %all-gather.15.cloned.1.call-update) | async-done | bytes 2097168 | tf_op jit(solution)/shard_map/all_gather | solution.py:67
  513.8 3.1 fusion.25
  517.0 0.0 copy-start.1
  517.0 0.0 copy-start.4
  517.0 0.0 copy-start.3
  517.0 0.0 reduce-scatter.6.cloned.1.call-update
  517.0 0.0 reduce-scatter.8.cloned.1.call-start
  517.0 5.4 all-to-all-done.1
  522.5 0.5 copy.19
  523.0 69.0 %psum.21 = f32[512]{0:T(512)} all-reduce(f32[512]{0:T(512)S(1)} %get-tuple-element.12), channel_id=1, replica_groups=mesh['tensor'=16,'shard'=16,'replica'=2] {'shard','replica'}, use_global_device_ids=true, to_apply=%region_8.0 | all-reduce | flops 512 | bytes 4096 | tf_op jit(solution)/shard_map/psum | solution.py:59
  592.0 9.8 %all-gather.17.cloned.1.call-done = bf16[2048,512]{1,0:T(8,128)(2,1)} async-done(((bf16[128,512]{1,0:T(8,128)(2,1)}), bf16[2048,512]{1,0:T(8,128)(2,1)}) %all-gather.17.cloned.1.call-update) | async-done | bytes 2097168 | tf_op jit(solution)/shard_map/all_gather | solution.py:66
  601.8 3.1 fusion.26
  604.9 0.0 reduce-scatter.8.cloned.1.call-update
  605.0 227.9 %reduce-scatter.4.cloned.1.call-done = f32[8,4096]{1,0:T(8,128)} async-done(((f32[128,4096]{1,0:T(8,128)}), f32[8,4096]{1,0:T(8,128)}) %reduce-scatter.4.cloned.1.call-update) | async-done | bytes 131088 | tf_op jit(solution)/shard_map/reduce_scatter | solution.py:52
  832.9 0.0 copy-done.1
  832.9 0.0 copy-done.4
  832.9 1.2 fusion.20
  834.1 99.9 %all-reduce = (f32[4096]{0:T(1024)}, f32[4096]{0:T(1024)}) all-reduce(f32[4096]{0:T(1024)S(1)} %get-tuple-element.6, f32[4096]{0:T(1024)S(1)} %get-tuple-element.9), channel_id=1, replica_groups=mesh['tensor'=16,'shard'=16,'replica'=2] {'tensor','shard','replica'}, use_global_device_ids=true, to_apply=%region_10.0 | all-reduce | flops 8192 | bytes 65536 | tf_op jit(solution)/shard_map/psum | solution.py:55
  934.0 0.0 copy-done.3
  934.0 1.6 fusion.19
  935.6 0.0 reduce-scatter.6.cloned.1.call-done
  935.6 0.0 reduce-scatter.8.cloned.1.call-done
  (3 shorter events, 0.0 us)
Async XLA Ops:
  7.2 405.4 %copy-start.5 = (f32[512]{0:T(512)S(1)}, f32[512]{0:T(512)}, u32[]{:S(2)}) copy-start(f32[512]{0:T(512)} %param.12) | copy-start | bytes 6148
  7.2 94.8 %all-gather.7.cloned.1.call-start = ((), (), s32[]{:S(2)}) async-start(), calls=%async_computation.5 | async-start | bytes 1114112 | tf_op jit(solution)/shard_map/all_gather | solution.py:44
  7.9 207.1 %all-gather.9.cloned.1.call-start = ((), (), s32[]{:S(2)}) async-start(), calls=%async_computation.6 | async-start | bytes 4456448 | tf_op jit(solution)/shard_map/all_gather | solution.py:47
  8.7 296.9 %all-gather.11.cloned.1.call-start = ((), (), s32[]{:S(2)}) async-start(), calls=%async_computation.7 | async-start | bytes 1114112 | tf_op jit(solution)/shard_map/all_gather | solution.py:43
  12.4 400.2 %all-gather.13.cloned.1.call-start = ((), (), s32[]{:S(2)}) async-start(), calls=%async_computation.8 | async-start | bytes 4456448 | tf_op jit(solution)/shard_map/all_gather | solution.py:46
  13.0 500.9 %all-gather.15.cloned.1.call-start = ((), (), s32[]{:S(2)}) async-start(), calls=%async_computation.10 | async-start | bytes 2228224 | tf_op jit(solution)/shard_map/all_gather | solution.py:67
  416.7 185.1 %all-gather.17.cloned.1.call-start = ((), (), s32[]{:S(2)}) async-start(), calls=%async_computation.12 | async-start | bytes 2228224 | tf_op jit(solution)/shard_map/all_gather | solution.py:66
  417.3 5.2 copy-start.2
  417.3 415.6 %reduce-scatter.4.cloned.1.call-start = ((), (), s32[]{:S(2)}) async-start(), calls=%async_computation.9 | async-start | bytes 2228224 | tf_op jit(solution)/shard_map/reduce_scatter | solution.py:52
  422.5 4.8 copy-start
  423.7 51.8 %all-to-all-start = ((bf16[128,16,256]{2,0,1:T(8,128)(2,1)}), bf16[128,16,256]{2,0,1:T(8,128)(2,1)S(1)}, u32[]{:S(2)}, u32[]{:S(2)}) async-start(bf16[128,16,256]{2,0,1:T(8,128)(2,1)} %bitcast.19), calls=%async_computation.1 | async-start | bytes 2097152 | tf_op jit(solution)/shard_map/all_to_all | solution.py:63
  475.5 47.0 %all-to-all-start.1 = ((bf16[128,16,256]{0,2,1:T(8,128)(2,1)}), bf16[128,16,256]{0,2,1:T(8,128)(2,1)S(1)}, u32[]{:S(2)}, u32[]{:S(2)}) async-start(bf16[128,16,256]{0,2,1:T(8,128)(2,1)} %bitcast.2), calls=%async_computation.3 | async-start | bytes 2097152 | tf_op jit(solution)/shard_map/all_to_all | solution.py:64
  479.9 455.7 %reduce-scatter.6.cloned.1.call-start = ((), (), s32[]{:S(2)}) async-start(), calls=%async_computation.11 | async-start | bytes 786432 | tf_op jit(solution)/shard_map/reduce_scatter | solution.py:71
  517.0 315.9 %copy-start.1 = (bf16[8,4096]{1,0:T(8,128)(2,1)S(1)}, bf16[8,4096]{1,0:T(8,128)(2,1)}, u32[]{:S(2)}) copy-start(bf16[8,4096]{1,0:T(8,128)(2,1)} %param.7) | copy-start | bytes 196612
  517.0 315.9 %copy-start.4 = (f32[4096]{0:T(1024)S(1)}, f32[4096]{0:T(1024)}, u32[]{:S(2)}) copy-start(f32[4096]{0:T(1024)} %param.9) | copy-start | bytes 49156
  517.0 417.0 %copy-start.3 = (bf16[8,4096]{1,0:T(8,128)(2,1)S(1)}, bf16[8,4096]{1,0:T(8,128)(2,1)}, u32[]{:S(2)}) copy-start(bf16[8,4096]{1,0:T(8,128)(2,1)} %param.8) | copy-start | bytes 196612
  517.0 418.6 %reduce-scatter.8.cloned.1.call-start = ((), (), s32[]{:S(2)}) async-start(), calls=%async_computation.13 | async-start | bytes 786432 | tf_op jit(solution)/shard_map/reduce_scatter | solution.py:72
Sparse Core Ops, SparseCore 0:
  11.2 90.7 all-gather.6
  104.0 111.0 all-gather.8
  218.8 86.7 all-gather.10
  307.5 105.0 all-gather.12
  416.8 96.9 all-gather.14
  516.4 85.4 all-gather.16
  606.3 226.5 reduce-scatter.3
  836.2 17.9 reduce-scatter.5
  857.8 17.3 reduce-scatter.7
where the time goes:
time: 943 us; the launch traced here: 942 us
  waiting for transfers between devices  722 us (77%)
  blocking collectives  169 us (18%)
  matrix products  19.6 us (2%)
  between operations  13.9 us (1%)
    reduce_scatter x1, waiting for transfers between devices, shards(): lax.psum_scatter(dot_nt(d_hidden, up_full), 'tensor', scatter_dimension=0...  228 us
    all_gather x1, waiting for transfers between devices, shards(): lax.all_gather(down_weight, 'shard', axis=1, tiled=True)  113 us
    all_gather x1, waiting for transfers between devices, shards(): up_full = lax.all_gather(up_weight, 'shard', axis=0, tiled=True)  107 us
    psum x1, blocking collectives, shards(): lax.psum((jnp.sum(d_normed * standard, axis=0), jnp.sum(d_normed, axis=0)...  99.9 us
    all_gather x1, waiting for transfers between devices, shards(): lax.all_gather(grad_out, 'tensor', axis=0, tiled=True)  88.9 us
    all_gather x1, waiting for transfers between devices, shards(): lax.all_gather(normed_local, 'tensor', axis=0, tiled=True)  86.5 us
    psum x1, blocking collectives, shards(): up_bias_grad = lax.psum(hidden_part, ('shard', 'replica'))  69 us
    all_to_all x1, waiting for transfers between devices, shards(): lax.all_to_all(normed, 'shard', split_axis=1, concat_axis=0, tiled=True)  46.8 us
  transfers between devices with their start and end apart: 11, of which 9 were waited for; matrix products, arithmetic and copies ran while one was open for 3% of the time, Pallas kernels for 0%

commit v1 on v0

--- a/solution.py
+++ b/solution.py
@@ -1,7 +1,190 @@
+import functools
 import jax
 import jax.numpy as jnp
 from jax import lax
+from jax.experimental import pallas as pl
+from jax.experimental.pallas import tpu as pltpu
 from jax.sharding import PartitionSpec as P
+
+MESH = pl.DeviceIdType.MESH
+NX, NY, NZ = 4, 4, 8
+
+
+class Links:
+    def __init__(self, send, recv):
+        self.send, self.recv, self.count, self.open = send, recv, 0, []
+
+    def push(self, src, dst, landed, device):
+        slot = self.count
+        self.count += 1
+        pltpu.make_async_remote_copy(
+            src_ref=src, dst_ref=dst, send_sem=self.send.at[slot], recv_sem=self.recv.at[slot],
+            device_id=device, device_id_type=MESH,
+        ).start()
+        arrival = pltpu.make_async_remote_copy(
+            src_ref=src, dst_ref=landed, send_sem=self.send.at[slot], recv_sem=self.recv.at[slot],
+            device_id=device, device_id_type=MESH,
+        )
+        self.open.append(arrival)
+        return arrival
+
+    def drain(self):
+        for arrival in self.open:
+            arrival.wait_send()
+        self.open = []
+
+
+def place():
+    t, s, c = lax.axis_index("tensor"), lax.axis_index("shard"), lax.axis_index("replica")
+    return t, s, c, s // NY, s % NY, t // NZ, t % NZ
+
+
+def greet(devices):
+    barrier = pltpu.get_barrier_semaphore()
+    for device in devices:
+        pl.semaphore_signal(barrier, inc=1, device_id=device, device_id_type=MESH)
+    pl.semaphore_wait(barrier, len(devices))
+
+
+def gather_kernel(rows_in, up_in, down_in, XG, WU, WD, raw, send, recv, local):
+    t, s, c, x, yl, yh, z = place()
+    sib = {"replica": 1 - c}
+    xdev = lambda k: {"shard": ((x + k) % NX) * NY + yl}
+    ydev = lambda k: {"shard": x * NY + (yl + k) % NY}
+    zdev = lambda k: {"tensor": yh * NZ + (z + k) % NZ}
+    opp = {"tensor": (1 - yh) * NZ + z}
+    sof = lambda dx, dy: ((x + dx + NX) % NX) * NY + (yl + dy + NY) % NY
+    tof = lambda dh, dz: ((yh + dh) % 2) * NZ + (z + dz + NZ) % NZ
+    net = Links(send, recv)
+
+    half = pl.multiple_of(c * 256, 256)
+    own_up, own_down = up_in.at[:, pl.ds(half, 256)], down_in.at[pl.ds(half, 256), :]
+    mine = [
+        pltpu.make_async_copy(own_up, WU.at[s], local.at[0]),
+        pltpu.make_async_copy(own_down, WD.at[s], local.at[1]),
+        pltpu.make_async_copy(rows_in, raw.at[c], local.at[2]),
+    ]
+    for copy in mine:
+        copy.start()
+    greet([sib, xdev(1), xdev(3), ydev(1), ydev(2), ydev(3), zdev(1), zdev(7), opp])
+
+    first = net.push(rows_in, raw.at[c], raw.at[1 - c], sib)
+    ych, xin = {}, {}
+    for k in (1, 2, 3):
+        ych[k] = (
+            net.push(own_up, WU.at[s], WU.at[sof(0, -k)], ydev(k)),
+            net.push(own_down, WD.at[s], WD.at[sof(0, -k)], ydev(k)),
+        )
+
+    def xsend(j):
+        here = sof(0, -j)
+        xin[j] = (
+            net.push(WU.at[here], WU.at[here], WU.at[sof(-1, -j)], xdev(1)),
+            net.push(WU.at[here], WU.at[here], WU.at[sof(1, -j)], xdev(3)),
+            net.push(WD.at[here], WD.at[here], WD.at[sof(-1, -j)], xdev(1)),
+            net.push(WD.at[here], WD.at[here], WD.at[sof(1, -j)], xdev(3)),
+        )
+
+    far = {}
+
+    def xforward(j):
+        left, right = sof(-1, -j), sof(1, -j)
+        for arrival in xin[j]:
+            arrival.wait_recv()
+        far[j] = (
+            net.push(WU.at[right], WU.at[right], WU.at[sof(2, -j)], xdev(3)),
+            net.push(WD.at[left], WD.at[left], WD.at[sof(2, -j)], xdev(1)),
+        )
+
+    twin = []
+
+    def share(slot, landed):
+        twin.append(net.push(XG.at[c, slot], XG.at[c, slot], XG.at[1 - c, landed], sib))
+
+    mine[0].wait()
+    mine[1].wait()
+    xsend(0)
+    mine[2].wait()
+    first.wait_recv()
+    for i in range(2):
+        XG[i, t] = jnp.concatenate([raw[0, i], raw[1, i]], axis=0).astype(jnp.bfloat16)
+    over = net.push(XG.at[c, t], XG.at[c, t], XG.at[c, tof(1, 0)], opp)
+
+    ring = {}
+
+    def zsend(q, k):
+        a, b = tof(q, -k), tof(q, k)
+        right = net.push(XG.at[c, a], XG.at[c, a], XG.at[c, tof(q, -k - 1)], zdev(1)) if k < 3 or q == 0 else None
+        left = net.push(XG.at[c, b], XG.at[c, b], XG.at[c, tof(q, k + 1)], zdev(7)) if k < 3 or q == 1 else None
+        ring[q, k] = (right, left)
+
+    def zland(q, k):
+        right, left = ring[q, k]
+        if right is not None:
+            right.wait_recv()
+        if left is not None:
+            left.wait_recv()
+        if k < 3:
+            zsend(q, k + 1)
+        if right is not None:
+            share(tof(q, -k - 1), tof(q, -k - 1))
+        if left is not None:
+            share(tof(q, k + 1), tof(q, k + 1))
+
+    def yland(j):
+        for arrival in ych[j]:
+            arrival.wait_recv()
+        xsend(j)
+
+    zsend(0, 0)
+    yland(1)
+    over.wait_recv()
+    zsend(1, 0)
+    share(tof(1, 0), tof(1, 0))
+    zland(0, 0)
+    yland(3)
+    zland(1, 0)
+    xforward(0)
+    zland(0, 1)
+    yland(2)
+    zland(1, 1)
+    xforward(1)
+    zland(0, 2)
+    zland(1, 2)
+    xforward(3)
+    zland(0, 3)
+    zland(1, 3)
+    xforward(2)
+    for j in (0, 1, 3, 2):
+        for arrival in far[j]:
+            arrival.wait_recv()
+    for arrival in twin:
+        arrival.wait_recv()
+    net.drain()
+
+
+def gather(rows, up_weight, down_weight):
+    vmem, any_ = pl.BlockSpec(memory_space=pltpu.VMEM), pl.BlockSpec(memory_space=pl.ANY)
+    bf = jnp.bfloat16
+    return pl.pallas_call(
+        gather_kernel,
+        out_shape=(
+            jax.ShapeDtypeStruct((2, 16, 16, 4096), bf),
+            jax.ShapeDtypeStruct((16, 256, 256), bf),
+            jax.ShapeDtypeStruct((16, 256, 256), bf),
+        ),
+        in_specs=[vmem, any_, any_],
+        out_specs=(vmem, vmem, vmem),
+        scratch_shapes=[
+            pltpu.VMEM((2, 2, 8, 4096), jnp.float32),
+            pltpu.SemaphoreType.DMA((80,)),
+            pltpu.SemaphoreType.DMA((80,)),
+            pltpu.SemaphoreType.DMA((3,)),
+        ],
+        compiler_params=pltpu.CompilerParams(
+            collective_id=0, has_side_effects=True, vmem_limit_bytes=40 << 20
+        ),
+    )(rows, up_weight, down_weight)
 
 
 def dot_nt(left, right):
@@ -39,38 +222,32 @@
 def shards(tokens, grad_out, norm_gain, norm_bias, up_weight, up_bias, down_weight):
     standard, inverse_std = normalize(tokens)
     normed_local = (standard * norm_gain + norm_bias).astype(jnp.bfloat16)
-    normed, grads_all = (
-        lax.all_gather(normed_local, "tensor", axis=0, tiled=True),
-        lax.all_gather(grad_out, "tensor", axis=0, tiled=True),
-    )
-    up_full = lax.all_gather(up_weight, "shard", axis=0, tiled=True)
-    d_act = dot_nt(grads_all, lax.all_gather(down_weight, "shard", axis=1, tiled=True))
-    pre_act = jnp.dot(normed, up_full, preferred_element_type=jnp.float32) + up_bias
+    rows = jnp.stack([normed_local.astype(jnp.float32), grad_out.astype(jnp.float32)])
+    XG, WU, WD = gather(rows, up_weight, down_weight)
+    c = lax.axis_index("replica")
+    normed, grads = XG[0].reshape(256, 4096), XG[1].reshape(256, 4096)
+    up_full = WU.reshape(4096, 256)
+    down_full = WD.transpose(1, 0, 2).reshape(256, 4096)
+    bias = lax.dynamic_slice_in_dim(up_bias, c * 256, 256)
+    d_act = dot_nt(grads, down_full)
+    pre_act = jnp.dot(normed, up_full, preferred_element_type=jnp.float32) + bias
     act = jax.nn.gelu(pre_act).astype(jnp.bfloat16)
     d_hidden = gelu_back(pre_act, d_act).astype(jnp.bfloat16)
     hidden_part = jnp.sum(d_hidden.astype(jnp.float32), axis=0)
-    d_normed = lax.psum_scatter(
-        dot_nt(d_hidden, up_full), "tensor", scatter_dimension=0, tiled=True
-    )
+    part = dot_nt(d_hidden, up_full).reshape(16, 2, 8, 4096).transpose(1, 0, 2, 3)
+    part = lax.psum_scatter(part, "replica", scatter_dimension=0, tiled=True)
+    d_normed = lax.psum_scatter(part.reshape(128, 4096), "tensor", scatter_dimension=0, tiled=True)
     gain_grad, bias_grad = lax.psum(
         (jnp.sum(d_normed * standard, axis=0), jnp.sum(d_normed, axis=0)),
         ("tensor", "shard", "replica"),
     )
-    up_bias_grad = lax.psum(hidden_part, ("shard", "replica"))
+    up_bias_grad = lax.all_gather(lax.psum(hidden_part, "shard"), "replica", axis=0, tiled=True)
     d_in = norm_back(d_normed, standard, inverse_std, norm_gain)
     input_grad = (grad_out.astype(jnp.float32) + d_in).astype(jnp.bfloat16)
-    normed_cols, grad_cols = (
-        lax.all_to_all(normed, "shard", split_axis=1, concat_axis=0, tiled=True),
-        lax.all_to_all(grads_all, "shard", split_axis=1, concat_axis=0, tiled=True),
-    )
-    act_piece = lax.all_gather(act, "shard", axis=0, tiled=True)
-    hidden_piece = lax.all_gather(d_hidden, "shard", axis=0, tiled=True)
-    up_part = dot_tn(normed_cols, hidden_piece)
-    down_part = dot_tn(act_piece, grad_cols)
-    up_grad, down_grad = (
-        lax.psum_scatter(up_part, "replica", scatter_dimension=0, tiled=True),
-        lax.psum_scatter(down_part, "replica", scatter_dimension=1, tiled=True),
-    )
+    up_part = lax.psum_scatter(dot_tn(normed, d_hidden), "shard", scatter_dimension=0, tiled=True)
+    down_part = lax.psum_scatter(dot_tn(act, grads), "shard", scatter_dimension=1, tiled=True)
+    up_grad = lax.all_to_all(up_part, "replica", split_axis=0, concat_axis=1, tiled=True)
+    down_grad = lax.all_to_all(down_part, "replica", split_axis=1, concat_axis=0, tiled=True)
     return (input_grad, up_grad, down_grad, up_bias_grad, gain_grad, bias_grad)
 
 

time: 943 us -> 642 us (0.68)
  waiting for transfers between devices: 722 us -> 355 us
  Pallas kernels: 0 us -> 64.7 us
  local copies, waits for them, and re-layouts: 2.98 us -> 21.6 us
    all_gather x6 -> x0, waiting for transfers between devices: 439 us -> none  [the longest x1 113 us: shards(): lax.all_gather(down_weight, 'shard', axis=1, tiled=True)]
    reduce_scatter x3, waiting for transfers between devices: 228 us -> 320 us  [the longest x1 213 us: shards(): lax.psum_scatter(part.reshape(128, 4096), 'tensor', scatter_dimension=0,...]
    pallas_call x0 -> x1, Pallas kernels: none -> 64.7 us  [gather(): pl.pallas_call(gather_kernel, out_shape=(jax.ShapeDtypeStruct((2, 16, 16,...]
    all_to_all x2 -> x0, waiting for transfers between devices: 52.3 us -> none  [the longest x1 46.8 us: shards(): lax.all_to_all(normed, 'shard', split_axis=1, concat_axis=0, tiled=True)]
    unnamed x9 -> x5, waiting for transfers between devices: 2.5 us -> 35.9 us
    psum x1, blocking collectives: 69 us -> 38.6 us  [shards(): lax.psum(hidden_part, 'shard')]
    all_to_all x0 -> x2, blocking collectives: none -> 18 us  [the longest x1 10.3 us: shards(): lax.all_to_all(up_part, 'replica', split_axis=0, concat_axis=1, tiled=True)]
    unnamed x12 -> x25, local copies, waits for them, and re-layouts: 0.02 us -> 9.61 us
  transfers between devices with their start and end apart: 11 -> 4, of which waited for: 9 -> 4; matrix products, arithmetic and copies ran while one was open for 3% -> 2% of each run, Pallas kernels for 0% -> 0%
where the time goes in v1:
time: 642 us; the launch traced here: 641 us
  waiting for transfers between devices  355 us (55%)
  blocking collectives  165 us (26%)
  Pallas kernels  64.7 us (10%)
  local copies, waits for them, and re-layouts  21.6 us (3%)
  between operations  15.7 us (2%)
  matrix products  11.5 us (2%)
  other arithmetic  6.72 us (1%)
    reduce_scatter x1, waiting for transfers between devices, shards(): lax.psum_scatter(part.reshape(128, 4096), 'tensor', scatter_dimension=0,...  213 us
    psum x1, blocking collectives, shards(): lax.psum((jnp.sum(d_normed * standard, axis=0), jnp.sum(d_normed, axis=0)...  101 us
    reduce_scatter x1, waiting for transfers between devices, shards(): lax.psum_scatter(dot_tn(normed, d_hidden), 'shard', scatter_dimension=0,...  95.9 us
    pallas_call x1, Pallas kernels, gather(): pl.pallas_call(gather_kernel, out_shape=(jax.ShapeDtypeStruct((2, 16, 16,...  64.7 us
    psum x1, blocking collectives, shards(): lax.psum(hidden_part, 'shard')  38.6 us
    unnamed x5, waiting for transfers between devices  35.9 us
  transfers between devices with their start and end apart: 4, of which 4 were waited for; matrix products, arithmetic and copies ran while one was open for 2% of the time, Pallas kernels for 0%

profile of v1, /device:TPU:1, one launch (start us, length us, event | category | flops | bytes accessed | tf_op | source)
XLA Modules:
  0.0 641.0 jit_solution(4653727502126208980)
XLA Ops:
  8.0 0.0 all-reduce.4.cloned.1.call-start
  8.0 1.0 convert_reduce_fusion.1
  9.0 1.1 fusion.19
  10.1 0.9 convert_bitcast_fusion
  11.0 0.9 fusion.27
  11.9 0.0 copy-start.1
  12.0 0.9 copy-done.1
  12.9 0.0 copy-start.2
  12.9 0.9 copy-done.2
  13.8 64.7 %shard_map.118 = (bf16[2,16,16,4096]{3,2,1,0:T(8,128)(2,1)S(1)}, bf16[16,256,256]{2,1,0:T(8,128)(2,1)S(1)}, bf16[16,256,256]{2,1,0:T(8,128)(2,1)S(1)}) custom-call(f32[2,8,4096]{2,1,0:T(8,128)S(1)} %pad_maximum_fusion.rows_in, bf16[256,512]{1,0:T(8,128)(2,1)S(1)} %copy-done.1, bf16[512,256]{1,0:T(8,128)(2,1)S(1)} %copy-done.2), custom_call_target="tpu_custom_call" | custom-call | tf_op jit(solution)/shard_map/pallas_call | solution.py:169
  78.5 0.0 copy-start
  78.5 1.9 copy-done
  80.4 0.0 copy-start.3
  80.4 1.3 copy-done.3
  81.8 2.4 copy.18
  84.2 0.0 copy-start.10
  84.2 4.0 fusion.33
  88.2 0.0 copy-done.10
  88.2 0.1 dynamic_slice.3
  88.3 0.0 copy-start.4
  88.3 0.0 copy-start.5
  88.3 2.4 fusion.34
  90.7 0.0 copy-done.4
  90.7 0.4 copy-done.5
  91.1 0.9 convert_reduce_fusion
  92.0 2.7 convolution_bitcast_fusion
  94.7 0.0 all-reduce.4.cloned.1.call-update
  94.7 0.0 reduce-scatter.9.cloned.1.call-start
  94.8 2.7 fusion.21
  97.5 0.0 copy-start.6
  97.5 0.0 reduce-scatter.9.cloned.1.call-update
  97.5 0.0 reduce-scatter.7.cloned.1.call-start
  97.6 1.5 copy-done.6
  99.1 2.7 fusion.35
  101.8 0.0 reduce-scatter.7.cloned.1.call-update
  101.9 0.0 reduce-scatter.5.cloned.1.call-start
  101.9 1.3 dynamic-slice
  103.2 35.8 %all-reduce.4.cloned.1.call-done = f32[2,16,8,4096]{3,2,0,1:T(8,128)} async-done(((f32[2,16,8,4096]{3,2,0,1:T(8,128)}), f32[2,16,8,4096]{3,2,0,1:T(8,128)}) %all-reduce.4.cloned.1.call-update) | async-done | bytes 4194320
  139.0 3.8 dynamic-slice_bitcast_fusion
  142.8 0.0 copy-start.7
  142.8 0.0 copy-start.9
  142.8 0.0 copy-start.8
  142.8 0.0 reduce-scatter.5.cloned.1.call-update
  142.8 38.6 %psum.21 = f32[256]{0:T(256)S(1)} all-reduce(f32[256]{0:T(256)S(1)} %get-tuple-element.18), channel_id=1, replica_groups=mesh['tensor'=16,'shard'=16,'replica'=2] {'shard'}, use_global_device_ids=true, to_apply=%region_9.0 | all-reduce | flops 256 | bytes 2048 | tf_op jit(solution)/shard_map/psum | solution.py:244
  181.4 7.9 %all-gather = f32[2,1,256]{2,1,0:T(1,128)S(1)} all-gather(f32[1,1,256]{2,1,0:T(1,128)S(1)} %bitcast.61), channel_id=1, replica_groups=mesh['tensor'=16,'shard'=16,'replica'=2] {'replica'}, dimensions={0}, use_global_device_ids=true | all-gather | bytes 3072 | tf_op jit(solution)/shard_map/all_gather | solution.py:244
  189.3 10.2 %reduce-scatter.9.cloned.1.call-done = f32[256,256]{1,0:T(8,128)} async-done(((f32[256,4096]{1,0:T(8,128)}), f32[256,256]{1,0:T(8,128)}) %reduce-scatter.9.cloned.1.call-update) | async-done | bytes 262160 | tf_op jit(solution)/shard_map/reduce_scatter | solution.py:248
  199.6 1.0 copy_bitcast_fusion
  200.6 7.6 %all_to_all.38 = f32[256,2,128]{2,0,1:T(8,128)S(1)} all-to-all(f32[256,2,128]{2,0,1:T(8,128)S(1)} %copy_bitcast_fusion), channel_id=1, replica_groups=mesh['tensor'=16,'shard'=16,'replica'=2] {'replica'}, dimensions={1} | all-to-all | bytes 524288 | tf_op jit(solution)/shard_map/all_to_all | solution.py:250
  208.2 95.9 %reduce-scatter.7.cloned.1.call-done = f32[256,256]{1,0:T(8,128)} async-done(((f32[4096,256]{1,0:T(8,128)}), f32[256,256]{1,0:T(8,128)}) %reduce-scatter.7.cloned.1.call-update) | async-done | bytes 262160 | tf_op jit(solution)/shard_map/reduce_scatter | solution.py:247
  304.1 10.3 %all_to_all.39 = f32[2,128,256]{2,1,0:T(8,128)S(1)} all-to-all(f32[2,128,256]{2,1,0:T(8,128)} %bitcast.57), channel_id=1, replica_groups=mesh['tensor'=16,'shard'=16,'replica'=2] {'replica'}, dimensions={0} | all-to-all | bytes 524288 | tf_op jit(solution)/shard_map/all_to_all | solution.py:249
  314.4 0.7 copy.25
  315.2 213.4 %reduce-scatter.5.cloned.1.call-done = f32[8,4096]{1,0:T(8,128)} async-done(((f32[128,4096]{1,0:T(8,128)}), f32[8,4096]{1,0:T(8,128)}) %reduce-scatter.5.cloned.1.call-update) | async-done | bytes 131088 | tf_op jit(solution)/shard_map/reduce_scatter | solution.py:239
  528.6 0.0 copy-done.7
  528.6 0.0 copy-done.9
  528.6 1.2 fusion.18
  529.8 100.7 %all-reduce.1 = (f32[4096]{0:T(1024)}, f32[4096]{0:T(1024)}) all-reduce(f32[4096]{0:T(1024)S(1)} %get-tuple-element.12, f32[4096]{0:T(1024)S(1)} %get-tuple-element.15), channel_id=1, replica_groups=mesh['tensor'=16,'shard'=16,'replica'=2] {'tensor','shard','replica'}, use_global_device_ids=true, to_apply=%region_11.0 | all-reduce | flops 8192 | bytes 65536 | tf_op jit(solution)/shard_map/psum | solution.py:240
  630.5 0.0 copy-done.8
  630.5 1.6 fusion.20
  632.1 0.7 copy.30
  632.8 0.6 copy.31
  (4 shorter events, 0.0 us)
Async XLA Ops:
  8.0 131.0 %all-reduce.4.cloned.1.call-start = ((), (), s32[]{:S(2)}) async-start(), calls=%async_computation.8 | async-start | bytes 8388608
  11.9 1.0 copy-start.1
  12.9 0.9 copy-start.2
  78.5 1.9 copy-start
  80.4 1.3 copy-start.3
  84.2 4.0 copy-start.10
  88.3 2.5 copy-start.4
  88.3 2.9 copy-start.5
  94.7 104.8 %reduce-scatter.9.cloned.1.call-start = ((), (), s32[]{:S(2)}) async-start(), calls=%async_computation.7 | async-start | bytes 4456448 | tf_op jit(solution)/shard_map/reduce_scatter | solution.py:248
  97.5 1.6 copy-start.6
  97.5 206.6 %reduce-scatter.7.cloned.1.call-start = ((), (), s32[]{:S(2)}) async-start(), calls=%async_computation.6 | async-start | bytes 4456448 | tf_op jit(solution)/shard_map/reduce_scatter | solution.py:247
  101.9 426.8 %reduce-scatter.5.cloned.1.call-start = ((), (), s32[]{:S(2)}) async-start(), calls=%async_computation.5 | async-start | bytes 2228224 | tf_op jit(solution)/shard_map/reduce_scatter | solution.py:239
  142.8 385.8 %copy-start.7 = (bf16[8,4096]{1,0:T(8,128)(2,1)S(1)}, bf16[8,4096]{1,0:T(8,128)(2,1)}, u32[]{:S(2)}) copy-start(bf16[8,4096]{1,0:T(8,128)(2,1)} %param.7) | copy-start | bytes 196612
  142.8 385.8 %copy-start.9 = (f32[4096]{0:T(1024)S(1)}, f32[4096]{0:T(1024)}, u32[]{:S(2)}) copy-start(f32[4096]{0:T(1024)} %param.9) | copy-start | bytes 49156
  142.8 487.7 %copy-start.8 = (bf16[8,4096]{1,0:T(8,128)(2,1)S(1)}, bf16[8,4096]{1,0:T(8,128)(2,1)}, u32[]{:S(2)}) copy-start(bf16[8,4096]{1,0:T(8,128)(2,1)} %param.8) | copy-start | bytes 196612
Sparse Core Ops, SparseCore 0:
  94.9 44.0 all-reduce.3
Sparse Core Ops, SparseCore 1:
  98.1 101.5 reduce-scatter.8
  202.3 101.8 reduce-scatter.6
  309.1 219.5 reduce-scatter.4

commit v2 on v1

--- a/solution.py
+++ b/solution.py
@@ -46,7 +46,18 @@
     pl.semaphore_wait(barrier, len(devices))
 
 
-def gather_kernel(rows_in, up_in, down_in, XG, WU, WD, raw, send, recv, local):
+def mm(left, right, dims):
+    return lax.dot_general(left, right, (dims, ((), ())), preferred_element_type=jnp.float32)
+
+
+def kernel(
+    tok_in, grad_in, gain_in, nbias_in, up_in, ubias_in, down_in,
+    dx_out, up_out, down_out, sums_out,
+    XG, WU, WD, raw, std, stdh, inv, act_t, dh, dh_t, pre, dact,
+    dxp, dxr, dxs, zr, zsum, hin, dn16, dn, gz, gh, gsum, gb, gy, gx,
+    P, CH, F, CE, DR, Y, YR, keep, ut, local, send, recv,
+):
+    bf, f32 = jnp.bfloat16, jnp.float32
     t, s, c, x, yl, yh, z = place()
     sib = {"replica": 1 - c}
     xdev = lambda k: {"shard": ((x + k) % NX) * NY + yl}
@@ -62,13 +73,11 @@
     mine = [
         pltpu.make_async_copy(own_up, WU.at[s], local.at[0]),
         pltpu.make_async_copy(own_down, WD.at[s], local.at[1]),
-        pltpu.make_async_copy(rows_in, raw.at[c], local.at[2]),
     ]
     for copy in mine:
         copy.start()
-    greet([sib, xdev(1), xdev(3), ydev(1), ydev(2), ydev(3), zdev(1), zdev(7), opp])
-
-    first = net.push(rows_in, raw.at[c], raw.at[1 - c], sib)
+    greet([sib, opp] + [xdev(k) for k in (1, 2, 3)] + [ydev(k) for k in (1, 2, 3)] + [zdev(k) for k in range(1, NZ)])
+
     ych, xin = {}, {}
     for k in (1, 2, 3):
         ych[k] = (
@@ -104,7 +113,18 @@
     mine[0].wait()
     mine[1].wait()
     xsend(0)
-    mine[2].wait()
+    wide = tok_in[...].astype(f32)
+    centred = wide - jnp.mean(wide, axis=-1, keepdims=True)
+    istd = lax.rsqrt(jnp.mean(centred * centred, axis=-1, keepdims=True) + 1e-05)
+    inv[...] = jnp.broadcast_to(istd, inv.shape)
+    std[...] = centred * istd
+    raw[c, 0] = (std[...] * gain_in[...] + nbias_in[...]).astype(bf).astype(f32)
+    raw[c, 1] = grad_in[...].astype(f32)
+    first = net.push(raw.at[c], raw.at[c], raw.at[1 - c], sib)
+    other_cols = pl.ds(pl.multiple_of((1 - c) * 2048, 2048), 2048)
+    my_cols = pl.ds(pl.multiple_of(c * 2048, 2048), 2048)
+    stdh[c] = std[:, my_cols]
+    std_in = net.push(std.at[:, other_cols], stdh.at[c], stdh.at[1 - c], sib)
     first.wait_recv()
     for i in range(2):
         XG[i, t] = jnp.concatenate([raw[0, i], raw[1, i]], axis=0).astype(jnp.bfloat16)
@@ -155,100 +175,250 @@
     zland(0, 3)
     zland(1, 3)
     xforward(2)
+
+    for arrival in twin:
+        arrival.wait_recv()
+
+    def forward(s1):
+        cols = pl.ds(pl.multiple_of(s1 * 256, 256), 256)
+        pre[...] += mm(XG[0, :, :, cols].reshape(256, 256), WU[s1], ((1,), (0,)))
+        dact[...] += mm(XG[1, :, :, cols].reshape(256, 256), WD[s1], ((1,), (1,)))
+
+    pre[...] = jnp.broadcast_to(ubias_in[pl.ds(c, 1), :], pre.shape)
+    dact[...] = jnp.zeros_like(dact)
+
+    @pl.loop(0, 16)
+    def _(s1):
+        @pl.when(s1 // NY != (x + 2) % NX)
+        def _():
+            forward(s1)
+
     for j in (0, 1, 3, 2):
         for arrival in far[j]:
             arrival.wait_recv()
-    for arrival in twin:
-        arrival.wait_recv()
+
+    @pl.loop(0, 4)
+    def _(y1):
+        forward(((x + 2) % NX) * NY + y1)
+
+    v = pre[...]
+    root = 0.7978845608028654
+    th = jnp.tanh(root * (v + 0.044715 * v * v * v))
+    act_t[...] = jnp.transpose(0.5 * v * (1.0 + th)).astype(bf)
+    slope = 0.5 * (1.0 + th) + 0.5 * v * (1.0 - th * th) * (root * (1.0 + 3 * 0.044715 * v * v))
+    grad_pre = (dact[...] * slope).astype(bf)
+    dh[...] = grad_pre
+    wide_pre = grad_pre.astype(f32)
+    dh_t[...] = jnp.transpose(wide_pre).astype(bf)
+    gb[...] = jnp.zeros_like(gb)
+    gb[8:9, 0:256] = jnp.sum(wide_pre, axis=0, keepdims=True)
+
+    @pl.loop(0, 8)
+    def _(i):
+        dxp[i] = mm(dh[...], WU[(1 - c) * 8 + i], ((1,), (1,))).astype(bf)
+
+    dx_in = net.push(dxp, dxr, dxr, sib)
+
+    chain, direct, ends, ysums = {}, {}, {}, {}
+
+    def partials(k):
+        @pl.loop(0, 4)
+        def _(i):
+            s1 = i * NY + (yl + k) % NY
+            cols = pl.ds(pl.multiple_of(s1 * 256, 256), 256)
+            P[0, s1] = mm(dh_t[...], XG[0, :, :, cols].reshape(256, 256), ((1,), (0,))).astype(bf)
+            P[1, s1] = mm(act_t[...], XG[1, :, :, cols].reshape(256, 256), ((1,), (0,))).astype(bf)
+
+        chain[k] = (
+            net.push(P.at[0, sof(2, k)], CH.at[0, k], CH.at[0, k], xdev(3)),
+            net.push(P.at[1, sof(2, k)], CH.at[1, k], CH.at[1, k], xdev(1)),
+        )
+        direct[k] = (
+            net.push(P.at[0, sof(1, k)], DR.at[0, k], DR.at[0, k], xdev(1)),
+            net.push(P.at[1, sof(-1, k)], DR.at[1, k], DR.at[1, k], xdev(3)),
+        )
+
+    def pass_on(k):
+        for u, (dx, device) in enumerate(((-1, xdev(3)), (1, xdev(1)))):
+            chain[k][u].wait_recv()
+            F[u, k] = (CH[u, k].astype(f32) + P[u, sof(dx, k)].astype(f32)).astype(bf)
+            ends[u, k] = net.push(F.at[u, k], CE.at[u, k], CE.at[u, k], device)
+
+    def finish_x(k):
+        for u in range(2):
+            direct[k][u].wait_recv()
+            ends[u, k].wait_recv()
+            total = P[u, sof(0, k)].astype(f32) + CE[u, k].astype(f32) + DR[u, k].astype(f32)
+            if k == 0:
+                keep[u] = total
+            else:
+                Y[u, k] = total.astype(bf)
+                ysums[u, k] = net.push(Y.at[u, k], YR.at[u, k], YR.at[u, k], ydev(k))
+
+    partials(2)
+    dx_in.wait_recv()
+
+    @pl.loop(0, 8)
+    def _(i):
+        total = mm(dh[...], WU[c * 8 + i], ((1,), (1,))) + dxr[i].astype(f32)
+        dxs[:, :, pl.ds(pl.multiple_of(i * 256, 256), 256)] = total.astype(bf).reshape(16, 16, 256)
+
+    zin = []
+    for k in (4, 3, 5, 2, 6, 1, 7):
+        for h in range(2):
+            zin.append(net.push(dxs.at[h * NZ + (z + k) % NZ], zr.at[k, h], zr.at[k, h], zdev(k)))
+    partials(1)
+    partials(3)
+    partials(0)
+    pass_on(2)
+    pass_on(1)
+    finish_x(2)
+    pass_on(3)
+
+    for arrival in zin:
+        arrival.wait_recv()
+
+    def zadd(h):
+        total = dxs[h * NZ + z].astype(f32)
+        for k in range(1, NZ):
+            total += zr[k, h].astype(f32)
+        return total
+
+    zsum[...] = zadd(1 - yh)
+    over = net.push(zsum, hin, hin, opp)
+    dn16[...] = zadd(yh)
+    finish_x(1)
+    pass_on(0)
+    over.wait_recv()
+    dn16[...] += hin[...]
+    rows_out = net.push(
+        dn16.at[pl.ds(pl.multiple_of((1 - c) * 8, 8), 8), :], dn.at[c], dn.at[1 - c], sib
+    )
+    dn[c] = dn16[pl.ds(pl.multiple_of(c * 8, 8), 8), :]
+    std_in.wait_recv()
+    shared = jnp.concatenate([stdh[0], stdh[1]], axis=0)
+    gsum_row = jnp.sum(dn16[...] * shared, axis=0, keepdims=True)
+    bsum_row = jnp.sum(dn16[...], axis=0, keepdims=True)
+    for i in range(4):
+        gsum[i : i + 1, :] = gsum_row[:, i * 512 : (i + 1) * 512]
+        gsum[4 + i : 5 + i, :] = bsum_row[:, i * 512 : (i + 1) * 512]
+    zg = [net.push(gsum, gz.at[k], gz.at[k], zdev(k)) for k in range(1, NZ)]
+    finish_x(3)
+    rows_out.wait_recv()
+    d_normed = jnp.concatenate([dn[0], dn[1]], axis=1)
+    scaled = d_normed * gain_in[...]
+    mean1 = jnp.mean(scaled, axis=-1, keepdims=True)
+    mean2 = jnp.mean(scaled * std[...], axis=-1, keepdims=True)
+    d_in = inv[:, 0:1] * (scaled - mean1 - std[...] * mean2)
+    dx_out[...] = (grad_in[...].astype(f32) + d_in).astype(bf)
+    total = gsum[...]
+    for k, arrival in enumerate(zg, 1):
+        arrival.wait_recv()
+        total += gz[k]
+    gb[0:8, :] = total
+    hg = net.push(gb.at[0:8, :], gh, gh, opp)
+    finish_x(0)
+    hg.wait_recv()
+    gy[0, 8:16, :] = gb[8:16, :]
+    gy[0, 0:8, :] = gb[0:8, :] + gh[...]
+    yg = [net.push(gy.at[0], gy.at[k], gy.at[k], ydev(k)) for k in (1, 2, 3)]
+    for arrival in yg:
+        arrival.wait_recv()
+    gx[0] = gy[0] + gy[1] + gy[2] + gy[3]
+    xg = [net.push(gx.at[0], gx.at[k], gx.at[k], xdev(k)) for k in (1, 2, 3)]
+    for u in range(2):
+        total = keep[u]
+        for k in (1, 2, 3):
+            ysums[u, k].wait_recv()
+            total += YR[u, k].astype(f32)
+        if u == 0:
+            total = jnp.transpose(total)
+        ut[u] = total
+    my_half, its_half = (pl.ds(pl.multiple_of(h * 128, 128), 128) for h in (c, 1 - c))
+    my_hid, its_hid = (pl.ds(pl.multiple_of(h * 256, 256), 256) for h in (c, 1 - c))
+    last = [
+        net.push(ut.at[0, its_half, :], up_out.at[:, my_hid], up_out.at[:, its_hid], sib),
+        net.push(ut.at[1, :, its_half], down_out.at[my_hid, :], down_out.at[its_hid, :], sib),
+    ]
+    mine = [
+        pltpu.make_async_copy(ut.at[0, my_half, :], up_out.at[:, my_hid], local.at[0]),
+        pltpu.make_async_copy(ut.at[1, :, my_half], down_out.at[my_hid, :], local.at[1]),
+    ]
+    for copy in mine:
+        copy.start()
+    for arrival in xg:
+        arrival.wait_recv()
+    sums_out[c] = gx[0] + gx[1] + gx[2] + gx[3]
+    last.append(net.push(sums_out.at[c], sums_out.at[c], sums_out.at[1 - c], sib))
+    for arrival in last:
+        arrival.wait_recv()
+    for copy in mine:
+        copy.wait()
     net.drain()
 
 
-def gather(rows, up_weight, down_weight):
+def shards(tokens, grad_out, norm_gain, norm_bias, up_weight, up_bias, down_weight):
     vmem, any_ = pl.BlockSpec(memory_space=pltpu.VMEM), pl.BlockSpec(memory_space=pl.ANY)
-    bf = jnp.bfloat16
-    return pl.pallas_call(
-        gather_kernel,
+    bf, f32 = jnp.bfloat16, jnp.float32
+    shape, room = jax.ShapeDtypeStruct, pltpu.VMEM
+    input_grad, up_grad, down_grad, sums = pl.pallas_call(
+        kernel,
         out_shape=(
-            jax.ShapeDtypeStruct((2, 16, 16, 4096), bf),
-            jax.ShapeDtypeStruct((16, 256, 256), bf),
-            jax.ShapeDtypeStruct((16, 256, 256), bf),
+            shape((8, 4096), bf), shape((128, 512), f32), shape((512, 128), f32), shape((2, 16, 512), f32),
         ),
-        in_specs=[vmem, any_, any_],
-        out_specs=(vmem, vmem, vmem),
+        in_specs=[vmem, vmem, vmem, vmem, any_, vmem, any_],
+        out_specs=(vmem, vmem, vmem, vmem),
         scratch_shapes=[
-            pltpu.VMEM((2, 2, 8, 4096), jnp.float32),
-            pltpu.SemaphoreType.DMA((80,)),
-            pltpu.SemaphoreType.DMA((80,)),
-            pltpu.SemaphoreType.DMA((3,)),
+            room((2, 16, 16, 4096), bf),
+            room((16, 256, 256), bf),
+            room((16, 256, 256), bf),
+            room((2, 2, 8, 4096), f32),
+            room((8, 4096), f32),
+            room((2, 8, 2048), f32),
+            room((8, 128), f32),
+            room((256, 256), bf),
+            room((256, 256), bf),
+            room((256, 256), bf),
+            room((256, 256), f32),
+            room((256, 256), f32),
+            room((8, 256, 256), bf),
+            room((8, 256, 256), bf),
+            room((16, 16, 2048), bf),
+            room((8, 2, 16, 2048), bf),
+            room((16, 2048), f32),
+            room((16, 2048), f32),
+            room((16, 2048), f32),
+            room((2, 8, 2048), f32),
+            room((8, 8, 512), f32),
+            room((8, 512), f32),
+            room((8, 512), f32),
+            room((16, 512), f32),
+            room((4, 16, 512), f32),
+            room((4, 16, 512), f32),
+            room((2, 16, 256, 256), bf),
+            room((2, 4, 256, 256), bf),
+            room((2, 4, 256, 256), bf),
+            room((2, 4, 256, 256), bf),
+            room((2, 4, 256, 256), bf),
+            room((2, 4, 256, 256), bf),
+            room((2, 4, 256, 256), bf),
+            room((2, 256, 256), f32),
+            room((2, 256, 256), f32),
+            pltpu.SemaphoreType.DMA((2,)),
+            pltpu.SemaphoreType.DMA((160,)),
+            pltpu.SemaphoreType.DMA((160,)),
         ],
         compiler_params=pltpu.CompilerParams(
-            collective_id=0, has_side_effects=True, vmem_limit_bytes=40 << 20
+            collective_id=0, has_side_effects=True, vmem_limit_bytes=50 << 20
         ),
-    )(rows, up_weight, down_weight)
-
-
-def dot_nt(left, right):
-    return lax.dot_general(
-        left, right, (((1,), (1,)), ((), ())), preferred_element_type=jnp.float32
+    )(
+        tokens, grad_out, norm_gain.reshape(1, 4096), norm_bias.reshape(1, 4096),
+        up_weight, up_bias.reshape(2, 256), down_weight,
     )
-
-
-def dot_tn(left, right):
-    return lax.dot_general(
-        left, right, (((0,), (0,)), ((), ())), preferred_element_type=jnp.float32
+    return (
+        input_grad, up_grad, down_grad, sums[:, 8, :256].reshape(512),
+        sums[:, 0:4].reshape(4096), sums[:, 4:8].reshape(4096),
     )
-
-
-def normalize(values):
-    widened = values.astype(jnp.float32)
-    centred = widened - jnp.mean(widened, axis=-1, keepdims=True)
-    variance = jnp.mean(centred * centred, axis=-1, keepdims=True)
-    inverse_std = lax.rsqrt(variance + 1e-05)
-    return (centred * inverse_std, inverse_std)
-
-
-def norm_back(d_normed, standard, inverse_std, gain):
-    scaled = d_normed * gain
-    first = jnp.mean(scaled, axis=-1, keepdims=True)
-    second = jnp.mean(scaled * standard, axis=-1, keepdims=True)
-    return inverse_std * (scaled - first - standard * second)
-
-
-def gelu_back(pre_act, upstream):
-    result, pull_back = jax.vjp(jax.nn.gelu, pre_act)
-    return pull_back(upstream)[0]
-
-
-def shards(tokens, grad_out, norm_gain, norm_bias, up_weight, up_bias, down_weight):
-    standard, inverse_std = normalize(tokens)
-    normed_local = (standard * norm_gain + norm_bias).astype(jnp.bfloat16)
-    rows = jnp.stack([normed_local.astype(jnp.float32), grad_out.astype(jnp.float32)])
-    XG, WU, WD = gather(rows, up_weight, down_weight)
-    c = lax.axis_index("replica")
-    normed, grads = XG[0].reshape(256, 4096), XG[1].reshape(256, 4096)
-    up_full = WU.reshape(4096, 256)
-    down_full = WD.transpose(1, 0, 2).reshape(256, 4096)
-    bias = lax.dynamic_slice_in_dim(up_bias, c * 256, 256)
-    d_act = dot_nt(grads, down_full)
-    pre_act = jnp.dot(normed, up_full, preferred_element_type=jnp.float32) + bias
-    act = jax.nn.gelu(pre_act).astype(jnp.bfloat16)
-    d_hidden = gelu_back(pre_act, d_act).astype(jnp.bfloat16)
-    hidden_part = jnp.sum(d_hidden.astype(jnp.float32), axis=0)
-    part = dot_nt(d_hidden, up_full).reshape(16, 2, 8, 4096).transpose(1, 0, 2, 3)
-    part = lax.psum_scatter(part, "replica", scatter_dimension=0, tiled=True)
-    d_normed = lax.psum_scatter(part.reshape(128, 4096), "tensor", scatter_dimension=0, tiled=True)
-    gain_grad, bias_grad = lax.psum(
-        (jnp.sum(d_normed * standard, axis=0), jnp.sum(d_normed, axis=0)),
-        ("tensor", "shard", "replica"),
-    )
-    up_bias_grad = lax.all_gather(lax.psum(hidden_part, "shard"), "replica", axis=0, tiled=True)
-    d_in = norm_back(d_normed, standard, inverse_std, norm_gain)
-    input_grad = (grad_out.astype(jnp.float32) + d_in).astype(jnp.bfloat16)
-    up_part = lax.psum_scatter(dot_tn(normed, d_hidden), "shard", scatter_dimension=0, tiled=True)
-    down_part = lax.psum_scatter(dot_tn(act, grads), "shard", scatter_dimension=1, tiled=True)
-    up_grad = lax.all_to_all(up_part, "replica", split_axis=0, concat_axis=1, tiled=True)
-    down_grad = lax.all_to_all(down_part, "replica", split_axis=1, concat_axis=0, tiled=True)
-    return (input_grad, up_grad, down_grad, up_bias_grad, gain_grad, bias_grad)
 
 
 def solution(mesh):

time: 642 us -> 150 us (0.23)
  waiting for transfers between devices: 355 us -> 0 us
  blocking collectives: 165 us -> 0 us
  Pallas kernels: 64.7 us -> 139 us
  between operations: 15.7 us -> 0.66 us
  local copies, waits for them, and re-layouts: 21.6 us -> 9.54 us
  matrix products: 11.5 us -> 0 us
  other arithmetic: 6.72 us -> 0 us
    reduce_scatter x3 -> x0, waiting for transfers between devices: 320 us -> none  [the longest x1 213 us: shards(): lax.psum_scatter(part.reshape(128, 4096), 'tensor', scatter_dimension=0,...]
    psum x2 -> x0, blocking collectives: 139 us -> none  [the longest x1 101 us: shards(): lax.psum((jnp.sum(d_normed * standard, axis=0), jnp.sum(d_normed, axis=0)...]
    pallas_call x1, Pallas kernels: 64.7 us -> 139 us  [shards(): pl.pallas_call(kernel, out_shape=(shape((8, 4096), bf), shape((128, 512),...]
    unnamed x5 -> x0, waiting for transfers between devices: 35.9 us -> none
    all_to_all x2 -> x0, blocking collectives: 18 us -> none  [the longest x1 10.3 us: shards(): lax.all_to_all(up_part, 'replica', split_axis=0, concat_axis=1, tiled=True)]
    dot_general x5 -> x0, matrix products: 11.5 us -> none  [the longest x2 5.44 us: dot_tn(): lax.dot_general(left, right, (((0,), (0,)), ((), ())), preferred_element_...]
    all_gather x1 -> x0, blocking collectives: 7.89 us -> none  [shards(): lax.all_gather(lax.psum(hidden_part, 'shard'), 'replica', axis=0, tiled=T...]
  transfers between devices with their start and end apart: 4 -> 0, of which waited for: 4 -> 0; matrix products, arithmetic and copies ran while one was open for 2% -> 0% of each run, Pallas kernels for 0% -> 0%
where the time goes in v2:
time: 150 us; the launch traced here: 149 us
  Pallas kernels  139 us (93%)
  local copies, waits for them, and re-layouts  9.54 us (6%)
    pallas_call x1, Pallas kernels, shards(): pl.pallas_call(kernel, out_shape=(shape((8, 4096), bf), shape((128, 512),...  139 us
    unnamed x20, local copies, waits for them, and re-layouts  8.95 us

profile of v2, /device:TPU:1, one launch (start us, length us, event | category | flops | bytes accessed | tf_op | source)
XLA Modules:
  0.0 149.5 jit_solution(3430223289053322062)
XLA Ops:
  0.6 0.0 copy-start.6
  0.6 0.7 copy-done.6
  1.3 0.0 copy-start
  1.3 0.9 copy-done
  2.3 0.0 copy-start.1
  2.3 0.9 copy-done.1
  3.2 0.0 copy-start.2
  3.2 0.8 copy-done.2
  4.1 0.0 copy-start.3
  4.1 0.8 copy-done.3
  4.9 0.0 copy-start.4
  4.9 0.7 copy-done.4
  5.6 0.0 copy-start.5
  5.6 0.7 copy-done.5
  6.3 139.3 %shard_map.118 = (bf16[8,4096]{1,0:T(8,128)(2,1)S(1)}, f32[128,512]{1,0:T(8,128)S(1)}, f32[512,128]{1,0:T(8,128)S(1)}, f32[2,16,512]{2,1,0:T(8,128)S(1)}) custom-call(bf16[8,4096]{1,0:T(8,128)(2,1)S(1)} %copy-done.2, bf16[8,4096]{1,0:T(8,128)(2,1)S(1)} %copy-done.3, f32[1,4096]{1,0:T(1,128)S(1)} %bitcast.9, f32[1,4096]{1,0:T(1,128)S(1)} %bitcast.10, ...), custom_call_target="tpu_custom_call" | custom-call | tf_op jit(solution)/shard_map/pallas_call | solution.py:364
  145.6 0.6 slice.9
  146.2 0.6 copy.14
  146.8 0.6 copy.13
  147.4 0.6 copy.18
  148.1 0.7 copy.19
  148.8 0.7 copy.20
  (2 shorter events, 0.0 us)
Async XLA Ops:
  0.6 0.7 copy-start.6
  1.3 0.9 copy-start
  2.3 0.9 copy-start.1
  3.2 0.8 copy-start.2
  4.1 0.8 copy-start.3
  4.9 0.7 copy-start.4
  5.6 0.7 copy-start.5

commit v3 on v2

v3 whole, which is shorter than its diff:
```python
import functools
import jax
import jax.numpy as jnp
from jax import lax
from jax.experimental import pallas as pl
from jax.experimental.pallas import tpu as pltpu
from jax.sharding import PartitionSpec as P

MESH = pl.DeviceIdType.MESH
NX, NY, NZ = 4, 4, 8


OFF = set()


def when(cond, body):
    if cond is None:
        body()
    else:
        pl.when(cond)(body)


class Nul:
    cond = None

    def wait_recv(self):
        pass

    def wait_send(self):
        pass


class Arrival:
    def __init__(self, copy, cond):
        self.copy, self.cond = copy, cond

    def wait_recv(self):
        when(self.cond, self.copy.wait_recv)

    def wait_send(self):
        when(self.cond, self.copy.wait_send)


class Links:
    def __init__(self, send, recv):
        self.send, self.recv, self.count, self.open = send, recv, 0, []

    def push(self, src, dst, landed, device, go=None, come=None):
        root = id(getattr(src, "ref", src))
        if self.groups.get(root, "D") in OFF:
            return Nul()
        slot = self.count
        self.count += 1
        pair = dict(
            send_sem=self.send.at[slot], recv_sem=self.recv.at[slot], device_id=device, device_id_type=MESH
        )
        when(go, pltpu.make_async_remote_copy(src_ref=src, dst_ref=dst, **pair).start)
        arrival = pltpu.make_async_remote_copy(src_ref=src, dst_ref=landed, **pair)
        self.open.append(Arrival(arrival, go))
        return Arrival(arrival, come)

    def drain(self):
        for arrival in self.open:
            arrival.wait_send()
        self.open = []


def place():
    t, s, c = lax.axis_index("tensor"), lax.axis_index("shard"), lax.axis_index("replica")
    return t, s, c, s // NY, s % NY, t // NZ, t % NZ


def greet(devices):
    barrier = pltpu.get_barrier_semaphore()
    for device in devices:
        pl.semaphore_signal(barrier, inc=1, device_id=device, device_id_type=MESH)
    pl.semaphore_wait(barrier, len(devices))


def mm(left, right, dims):
    return lax.dot_general(left, right, (dims, ((), ())), preferred_element_type=jnp.float32)


def kernel(
    tok_in, grad_in, gain_hbm, nbias_hbm, up_in, ubias_hbm, down_in,
    dx_out, up_out, down_out, sums_out,
    XG, XN, WU, WD, gain, nbias, ubias, raw, std, inv, mu, iv, act_t, dh, dh_t, pre, dact,
    dxp, dxr, dxs, zr, zsum, hin, dn16, dn, gz, gh, gsum, gb, gy, gx,
    P, CH, F, CE, DR, Y, YR, keep, ut, local, send, recv,
):
    bf, f32 = jnp.bfloat16, jnp.float32
    t, s, c, x, yl, yh, z = place()
    sib = {"replica": 1 - c}
    xdev = lambda k: {"shard": ((x + k) % NX) * NY + yl}
    ydev = lambda k: {"shard": x * NY + (yl + k) % NY}
    zdev = lambda k: {"tensor": yh * NZ + (z + k) % NZ}
    opp = {"tensor": (1 - yh) * NZ + z}
    sof = lambda dx, dy: ((x + dx + NX) % NX) * NY + (yl + dy + NY) % NY
    tof = lambda dh, dz: ((yh + dh) % 2) * NZ + (z + dz + NZ) % NZ
    net = Links(send, recv)
    root_of = lambda ref: id(getattr(ref, "ref", ref))
    net.groups = {root_of(r): g for g, rs in {"W": (up_in, down_in, WU, WD), "Z": (XG, raw), "X": (P, F, Y, ut)}.items() for r in rs}

    half = pl.multiple_of(c * 256, 256)
    own_up, own_down = up_in.at[:, pl.ds(half, 256)], down_in.at[pl.ds(half, 256), :]
    mine = [
        pltpu.make_async_copy(own_up, WU.at[s], local.at[0]),
        pltpu.make_async_copy(own_down, WD.at[s], local.at[1]),
        pltpu.make_async_copy(gain_hbm, gain, local.at[2]),
        pltpu.make_async_copy(nbias_hbm, nbias, local.at[3]),
        pltpu.make_async_copy(ubias_hbm, ubias, local.at[4]),
    ]
    for copy in mine:
        copy.start()
    raw[c, 0] = tok_in[...].astype(f32)
    raw[c, 1] = grad_in[...].astype(f32)
    greet([sib, opp] + [xdev(k) for k in (1, 2, 3)] + [ydev(k) for k in (1, 2, 3)] + [zdev(k) for k in range(1, NZ)])
    first = net.push(raw.at[c], raw.at[c], raw.at[1 - c], sib)
    mine[0].wait()
    mine[1].wait()

    has_left, has_right = yl > 0, yl < NY - 1
    line, xin, far = {}, {}, {}

    def there(side, k):
        return yl - 1 - k >= 0 if side < 0 else yl + 1 + k <= NY - 1

    def along(side, k):
        here, landed = sof(0, side * k), sof(0, side * (k + 1))
        if side < 0:
            go = has_right if k == 0 else jnp.logical_and(has_right, yl - k >= 0)
        else:
            go = has_left if k == 0 else jnp.logical_and(has_left, yl + k <= NY - 1)
        line[side, k] = [
            net.push(w.at[here], w.at[here], w.at[landed], ydev(1 if side < 0 else 3), go, there(side, k))
            for w in (WU, WD)
        ]

    def xsend(name, dy, cond):
        here, left, right = sof(0, dy), sof(-1, dy), sof(1, dy)
        xin[name] = [
            net.push(WU.at[here], WU.at[here], WU.at[right], xdev(3), cond, cond),
            net.push(WD.at[here], WD.at[here], WD.at[left], xdev(1), cond, cond),
            net.push(WU.at[here], WU.at[here], WU.at[left], xdev(1), cond, cond),
            net.push(WD.at[here], WD.at[here], WD.at[right], xdev(3), cond, cond),
        ]

    def xforward(name, dy, cond):
        left, right, opposite = sof(-1, dy), sof(1, dy), sof(2, dy)
        xin[name][0].wait_recv()
        one = net.push(WU.at[right], WU.at[right], WU.at[opposite], xdev(3), cond, cond)
        xin[name][1].wait_recv()
        two = net.push(WD.at[left], WD.at[left], WD.at[opposite], xdev(1), cond, cond)
        xin[name][2].wait_recv()
        xin[name][3].wait_recv()
        far[name] = (one, two)

    def yland(k):
        for side in (-1, 1):
            for arrival in line[side, k]:
                arrival.wait_recv()
            if k < 2:
                along(side, k + 1)
            xsend((side, k), side * (k + 1), there(side, k))

    def pass_x(k):
        for side in (-1, 1):
            xforward((side, k), side * (k + 1), there(side, k))

    along(-1, 0)
    along(1, 0)
    xsend("own", 0, None)

    twin, ring = {}, {}

    def share(name, slot):
        twin.setdefault(name, []).append(net.push(XG.at[c, slot], XG.at[c, slot], XG.at[1 - c, slot], sib))

    def zsend(q, k):
        a, b = tof(q, -k), tof(q, k)
        right = net.push(XG.at[c, a], XG.at[c, a], XG.at[c, tof(q, -k - 1)], zdev(1)) if k < 3 or q == 0 else None
        left = net.push(XG.at[c, b], XG.at[c, b], XG.at[c, tof(q, k + 1)], zdev(7)) if k < 3 or q == 1 else None
        ring[q, k] = (right, left)

    def zland(q, k):
        right, left = ring[q, k]
        if right is not None:
            right.wait_recv()
        if left is not None:
            left.wait_recv()
        if k < 3:
            zsend(q, k + 1)
        if right is not None:
            share(k, tof(q, -k - 1))
        if left is not None:
            share(k, tof(q, k + 1))

    def normalize(slot):
        wide = XG[0, slot].astype(f32)
        mean = jnp.mean(wide, axis=-1, keepdims=True)
        centred = wide - mean
        istd = lax.rsqrt(jnp.mean(centred * centred, axis=-1, keepdims=True) + 1e-05)
        XN[slot] = (centred * istd * gain[...] + nbias[...]).astype(bf)
        mu[slot] = jnp.broadcast_to(mean, (16, 128))
        iv[slot] = jnp.broadcast_to(istd, (16, 128))

    def settle(k):
        for arrival in twin[k]:
            arrival.wait_recv()
        if k == "y":
            normalize(tof(1, 0))
        elif k < 3:

            @pl.loop(0, 4)
            def _(i):
                normalize(((yh + i // 2) % 2) * NZ + (z + (2 * (i % 2) - 1) * (k + 1) + NZ) % NZ)
        else:

            @pl.loop(0, 2)
            def _(i):
                normalize(((yh + i) % 2) * NZ + (z + 4) % NZ)

    first.wait_recv()
    for i in range(2):
        XG[i, t] = jnp.concatenate([raw[0, i], raw[1, i]], axis=0).astype(bf)
    over = net.push(XG.at[c, t], XG.at[c, t], XG.at[c, tof(1, 0)], opp)
    zsend(0, 0)
    for copy in mine[2:]:
        copy.wait()
    normalize(t)
    yland(0)
    over.wait_recv()
    zsend(1, 0)
    share("y", tof(1, 0))
    zland(0, 0)
    xforward("own", 0, None)
    zland(1, 0)
    yland(1)
    settle("y")
    zland(0, 1)
    pass_x(0)
    zland(1, 1)
    yland(2)
    settle(0)
    zland(0, 2)
    zland(1, 2)
    settle(1)
    pass_x(1)
    zland(0, 3)
    zland(1, 3)
    settle(2)
    wide = raw[c, 0]
    centred = wide - jnp.mean(wide, axis=-1, keepdims=True)
    istd = lax.rsqrt(jnp.mean(centred * centred, axis=-1, keepdims=True) + 1e-05)
    inv[...] = jnp.broadcast_to(istd, inv.shape)
    std[...] = centred * istd
    settle(3)

    def forward(s1):
        cols = pl.ds(pl.multiple_of(s1 * 256, 256), 256)
        pre[...] += mm(XN[:, :, cols].reshape(256, 256), WU[s1], ((1,), (0,)))
        dact[...] += mm(XG[1, :, :, cols].reshape(256, 256), WD[s1], ((1,), (1,)))

    pre[...] = jnp.broadcast_to(ubias[:, pl.ds(half, 256)], pre.shape)
    dact[...] = jnp.zeros_like(dact)
    remote = lambda y1: jnp.abs(y1 - yl) == 3
    near = lambda i, y1: ((x + i + i // 2) % NX) * NY + y1

    @pl.loop(0, 12)
    def _(i):
        @pl.when(jnp.logical_not(remote(i // 3)))
        def _():
            forward(near(i % 3, i // 3))

    pass_x(2)
    for name in ("own", (-1, 0), (1, 0), (-1, 1), (1, 1)):
        for arrival in far[name]:
            arrival.wait_recv()

    @pl.loop(0, 4)
    def _(y1):
        @pl.when(jnp.logical_not(remote(y1)))
        def _():
            forward(((x + 2) % NX) * NY + y1)

    ends_line = jnp.logical_or(yl == 0, yl == 3)

    @pl.when(ends_line)
    def _():
        @pl.loop(0, 3)
        def _(i):
            forward(near(i, 3 - yl))

    for name in ((-1, 2), (1, 2)):
        for arrival in far[name]:
            arrival.wait_recv()

    @pl.when(ends_line)
    def _():
        forward(((x + 2) % NX) * NY + 3 - yl)

    v = pre[...]
    root = 0.7978845608028654
    th = jnp.tanh(root * (v + 0.044715 * v * v * v))
    slope = 0.5 * (1.0 + th) + 0.5 * v * (1.0 - th * th) * (root * (1.0 + 3 * 0.044715 * v * v))
    grad_pre = (dact[...] * slope).astype(bf)
    dh[...] = grad_pre

    @pl.loop(0, 8)
    def _(i):
        dxp[i] = mm(dh[...], WU[(1 - c) * 8 + i], ((1,), (1,))).astype(bf)

    dx_in = net.push(dxp, dxr, dxr, sib)
    wide_pre = grad_pre.astype(f32)
    dh_t[...] = jnp.transpose(wide_pre).astype(bf)
    act_t[...] = jnp.transpose(0.5 * v * (1.0 + th)).astype(bf)
    gb[16:24, :] = jnp.broadcast_to(jnp.sum(wide_pre, axis=0, keepdims=True), (8, 256))

    chain, direct, ends, ysums = {}, {}, {}, {}

    def partials(k):
        @pl.loop(0, 4)
        def _(i):
            s1 = i * NY + (yl + k) % NY
            cols = pl.ds(pl.multiple_of(s1 * 256, 256), 256)
            P[0, s1] = mm(dh_t[...], XN[:, :, cols].reshape(256, 256), ((1,), (0,))).astype(bf)
            P[1, s1] = mm(act_t[...], XG[1, :, :, cols].reshape(256, 256), ((1,), (0,))).astype(bf)

        chain[k] = (
            net.push(P.at[0, sof(2, k)], CH.at[0, k], CH.at[0, k], xdev(3)),
            net.push(P.at[1, sof(2, k)], CH.at[1, k], CH.at[1, k], xdev(1)),
        )
        direct[k] = (
            net.push(P.at[0, sof(1, k)], DR.at[0, k], DR.at[0, k], xdev(1)),
            net.push(P.at[1, sof(-1, k)], DR.at[1, k], DR.at[1, k], xdev(3)),
        )

    def pass_on(k):
        for u, (dx, device) in enumerate(((-1, xdev(3)), (1, xdev(1)))):
            chain[k][u].wait_recv()
            F[u, k] = (CH[u, k].astype(f32) + P[u, sof(dx, k)].astype(f32)).astype(bf)
            ends[u, k] = net.push(F.at[u, k], CE.at[u, k], CE.at[u, k], device)

    def finish_x(k):
        for u in range(2):
            direct[k][u].wait_recv()
            ends[u, k].wait_recv()
            total = P[u, sof(0, k)].astype(f32) + CE[u, k].astype(f32) + DR[u, k].astype(f32)
            if k == 0:
                keep[u] = total
            else:
                Y[u, k] = total.astype(bf)
                ysums[u, k] = net.push(Y.at[u, k], YR.at[u, k], YR.at[u, k], ydev(k))

    partials(2)
    dx_in.wait_recv()

    @pl.loop(0, 8)
    def _(i):
        total = mm(dh[...], WU[c * 8 + i], ((1,), (1,))) + dxr[i].astype(f32)
        dxs[:, :, pl.ds(pl.multiple_of(i * 256, 256), 256)] = total.astype(bf).reshape(16, 16, 256)
        cols = pl.ds(pl.multiple_of((c * 8 + i) * 256, 256), 256)
        tok = XG[0, :, :, cols].reshape(256, 256).astype(f32)
        standard = (tok - mu[...].reshape(256, 128)[:, 0:1]) * iv[...].reshape(256, 128)[:, 0:1]
        gsum[pl.ds(i, 1), :] = jnp.sum(total * standard, axis=0, keepdims=True)
        gsum[pl.ds(8 + i, 1), :] = jnp.sum(total, axis=0, keepdims=True)

    zg = [net.push(gsum, gz.at[k], gz.at[k], zdev(k)) for k in range(1, NZ)]
    zin = []
    for k in (4, 3, 5, 2, 6, 1, 7):
        for h in range(2):
            zin.append(net.push(dxs.at[h * NZ + (z + k) % NZ], zr.at[k, h], zr.at[k, h], zdev(k)))
    partials(1)
    pass_on(2)
    partials(3)
    pass_on(1)
    finish_x(2)
    partials(0)
    total = gsum[...]
    for k, arrival in enumerate(zg, 1):
        arrival.wait_recv()
        total += gz[k]
    gb[0:16, :] = total
    hg = net.push(gb.at[0:16, :], gh, gh, opp)
    pass_on(3)
    finish_x(1)
    hg.wait_recv()
    gy[0, 16:24, :] = gb[16:24, :]
    gy[0, 0:16, :] = gb[0:16, :] + gh[...]
    yg = [net.push(gy.at[0], gy.at[k], gy.at[k], ydev(k)) for k in (1, 2, 3)]

    for arrival in zin:
        arrival.wait_recv()

    def zadd(h):
        total = dxs[h * NZ + z].astype(f32)
        for k in range(1, NZ):
            total += zr[k, h].astype(f32)
        return total

    zsum[...] = zadd(1 - yh)
    over = net.push(zsum, hin, hin, opp)
    dn16[...] = zadd(yh)
    pass_on(0)
    finish_x(3)
    for arrival in yg:
        arrival.wait_recv()
    gx[0] = gy[0] + gy[1] + gy[2] + gy[3]
    xg = [net.push(gx.at[0], gx.at[k], gx.at[k], xdev(k)) for k in (1, 2, 3)]
    over.wait_recv()
    dn16[...] += hin[...]
    rows_out = net.push(
        dn16.at[pl.ds(pl.multiple_of((1 - c) * 8, 8), 8), :], dn.at[c], dn.at[1 - c], sib
    )
    dn[c] = dn16[pl.ds(pl.multiple_of(c * 8, 8), 8), :]
    for arrival in xg:
        arrival.wait_recv()
    sums_out[c] = gx[0] + gx[1] + gx[2] + gx[3]
    last = [net.push(sums_out.at[c], sums_out.at[c], sums_out.at[1 - c], sib)]
    rows_out.wait_recv()
    d_normed = jnp.concatenate([dn[0], dn[1]], axis=1)
    scaled = d_normed * gain[...]
    mean1 = jnp.mean(scaled, axis=-1, keepdims=True)
    mean2 = jnp.mean(scaled * std[...], axis=-1, keepdims=True)
    d_in = inv[:, 0:1] * (scaled - mean1 - std[...] * mean2)
    dx_out[...] = (raw[c, 1] + d_in).astype(bf)
    finish_x(0)
    for u in range(2):
        total = keep[u]
        for k in (1, 2, 3):
            ysums[u, k].wait_recv()
            total += YR[u, k].astype(f32)
        if u == 0:
            total = jnp.transpose(total)
        ut[u] = total
    my_half, its_half = (pl.ds(pl.multiple_of(h * 128, 128), 128) for h in (c, 1 - c))
    my_hid, its_hid = (pl.ds(pl.multiple_of(h * 256, 256), 256) for h in (c, 1 - c))
    last += [
        net.push(ut.at[0, its_half, :], up_out.at[:, my_hid], up_out.at[:, its_hid], sib),
        net.push(ut.at[1, :, its_half], down_out.at[my_hid, :], down_out.at[its_hid, :], sib),
    ]
    mine = [
        pltpu.make_async_copy(ut.at[0, my_half, :], up_out.at[:, my_hid], local.at[0]),
        pltpu.make_async_copy(ut.at[1, :, my_half], down_out.at[my_hid, :], local.at[1]),
    ]
    for copy in mine:
        copy.start()
    for arrival in last:
        arrival.wait_recv()
    for copy in mine:
        copy.wait()
    net.drain()


def shards(tokens, grad_out, norm_gain, norm_bias, up_weight, up_bias, down_weight):
    vmem, hbm = pl.BlockSpec(memory_space=pltpu.VMEM), pl.BlockSpec(memory_space=pltpu.HBM)
    bf, f32 = jnp.bfloat16, jnp.float32
    shape, room = jax.ShapeDtypeStruct, pltpu.VMEM
    input_grad, up_grad, down_grad, sums = pl.pallas_call(
        kernel,
        out_shape=(
            shape((8, 4096), bf), shape((128, 512), f32), shape((512, 128), f32), shape((2, 24, 256), f32),
        ),
        in_specs=[vmem, vmem, hbm, hbm, hbm, hbm, hbm],
        out_specs=(vmem, vmem, vmem, vmem),
        scratch_shapes=[
            room((2, 16, 16, 4096), bf),
            room((16, 16, 4096), bf),
            room((16, 256, 256), bf),
            room((16, 256, 256), bf),
            room((1, 4096), f32),
            room((1, 4096), f32),
            room((1, 512), f32),
            room((2, 2, 8, 4096), f32),
            room((8, 4096), f32),
            room((8, 128), f32),
            room((16, 16, 128), f32),
            room((16, 16, 128), f32),
            room((256, 256), bf),
            room((256, 256), bf),
            room((256, 256), bf),
            room((256, 256), f32),
            room((256, 256), f32),
            room((8, 256, 256), bf),
            room((8, 256, 256), bf),
            room((16, 16, 2048), bf),
            room((8, 2, 16, 2048), bf),
            room((16, 2048), f32),
            room((16, 2048), f32),
            room((16, 2048), f32),
            room((2, 8, 2048), f32),
            room((8, 16, 256), f32),
            room((16, 256), f32),
            room((16, 256), f32),
            room((24, 256), f32),
            room((4, 24, 256), f32),
            room((4, 24, 256), f32),
            room((2, 16, 256, 256), bf),
            room((2, 4, 256, 256), bf),
            room((2, 4, 256, 256), bf),
            room((2, 4, 256, 256), bf),
            room((2, 4, 256, 256), bf),
            room((2, 4, 256, 256), bf),
            room((2, 4, 256, 256), bf),
            room((2, 256, 256), f32),
            room((2, 256, 256), f32),
            pltpu.SemaphoreType.DMA((5,)),
            pltpu.SemaphoreType.DMA((180,)),
            pltpu.SemaphoreType.DMA((180,)),
        ],
        compiler_params=pltpu.CompilerParams(
            collective_id=0, has_side_effects=True, vmem_limit_bytes=63 << 20
        ),
    )(
        tokens, grad_out, norm_gain.reshape(1, 4096), norm_bias.reshape(1, 4096),
        up_weight, up_bias.reshape(1, 512), down_weight,
    )
    return (
        input_grad, up_grad, down_grad, sums[:, 16].reshape(512),
        sums[:, 0:8].reshape(4096), sums[:, 8:16].reshape(4096),
    )


def solution(mesh):
    return jax.shard_map(
        shards,
        mesh=mesh,
        in_specs=(
            P(("tensor", "shard", "replica"), None),
            P(("tensor", "shard", "replica"), None),
            P(),
            P(),
            P("shard", "tensor"),
            P("tensor"),
            P("tensor", "shard"),
        ),
        out_specs=(
            P(("tensor", "shard", "replica"), None),
            P(("shard", "replica"), "tensor"),
            P("tensor", ("shard", "replica")),
            P("tensor"),
            P(),
            P(),
        ),
        check_vma=False,
    )
```

time: 150 us -> 126 us (0.84)
  the two profiles are of different devices: /device:TPU:1 before, /device:TPU:25 now
where the time goes in v3:
time: 126 us
  Pallas kernels  118 us (94%)
  local copies, waits for them, and re-layouts  6.53 us (5%)
    pallas_call x1, Pallas kernels, shards(): pl.pallas_call(kernel, out_shape=(shape((8, 4096), bf), shape((128, 512),...  118 us
    unnamed x10, local copies, waits for them, and re-layouts  5.19 us

profile of v3, /device:TPU:25, one launch (start us, length us, event | category | flops | bytes accessed | tf_op | source)
XLA Modules:
  0.0 125.6 jit_solution(18225289870202151329)
XLA Ops:
  0.6 118.5 %shard_map.118 = (bf16[8,4096]{1,0:T(8,128)(2,1)}, f32[128,512]{1,0:T(8,128)}, f32[512,128]{1,0:T(8,128)}, f32[2,24,256]{2,1,0:T(8,128)}) custom-call(bf16[8,4096]{1,0:T(8,128)(2,1)} %tok_in.1, bf16[8,4096]{1,0:T(8,128)(2,1)} %grad_in.1, f32[1,4096]{1,0:T(1,128)} %bitcast.10, f32[1,4096]{1,0:T(1,128)} %bitcast.11, bf16[256,512]{1,0:T(8,128)(2,1)} %up_in.1, ...), custom_call_target="tpu_custom_call" | custom-call | tf_op jit(solution)/shard_map/pallas_call | solution.py:459
  119.1 0.0 copy-start.1
  119.1 1.3 %slice.9 = f32[2,1,256]{2,1,0:T(1,128)} slice(f32[2,24,256]{2,1,0:T(8,128)} %get-tuple-element.13), slice={[0:2], [16:17], [0:256]} | slice | bytes 4096 | tf_op jit(solution)/shard_map/slice | solution.py:519
  120.4 0.7 slice_bitcast_fusion
  121.2 0.6 copy.14
  121.8 0.6 copy.13
  122.4 1.5 %copy.18 = bf16[8,4096]{1,0:T(8,128)(2,1)} copy(bf16[8,4096]{1,0:T(8,128)(2,1)} %get-tuple-element.22) | data formatting | bytes 131072
  123.9 0.0 copy-done.1
  123.9 0.0 copy-start
  123.9 0.7 copy.19
  124.6 0.3 copy-done
  124.9 0.7 copy.20
Async XLA Ops:
  119.1 4.8 %copy-start.1 = (f32[128,512]{1,0:T(8,128)S(1)}, f32[128,512]{1,0:T(8,128)}, u32[]{:S(2)}) copy-start(f32[128,512]{1,0:T(8,128)} %get-tuple-element.23) | copy-start | bytes 786436
  123.9 1.0 copy-start

commit v4 on v3

--- a/solution.py
+++ b/solution.py
@@ -83,10 +83,10 @@
 
 def kernel(
     tok_in, grad_in, gain_hbm, nbias_hbm, up_in, ubias_hbm, down_in,
-    dx_out, up_out, down_out, sums_out,
+    dx_out, up_out, down_out, ub_out, gg_out, bg_out,
     XG, XN, WU, WD, gain, nbias, ubias, raw, std, inv, mu, iv, act_t, dh, dh_t, pre, dact,
     dxp, dxr, dxs, zr, zsum, hin, dn16, dn, gz, gh, gsum, gb, gy, gx,
-    P, CH, F, CE, DR, Y, YR, keep, ut, local, send, recv,
+    P, CH, F, CE, DR, Y, YR, keep, ut, sums, local, send, recv,
 ):
     bf, f32 = jnp.bfloat16, jnp.float32
     t, s, c, x, yl, yh, z = place()
@@ -173,27 +173,31 @@
 
     twin, ring = {}, {}
 
-    def share(name, slot):
-        twin.setdefault(name, []).append(net.push(XG.at[c, slot], XG.at[c, slot], XG.at[1 - c, slot], sib))
-
-    def zsend(q, k):
+    def part(i, slot, h):
+        return XG.at[i, slot, :, pl.ds(h * 2048, 2048)]
+
+    def share(name, slot, h):
+        twin.setdefault(name, []).append(net.push(part(c, slot, h), part(c, slot, h), part(1 - c, slot, h), sib))
+
+    def zsend(q, k, h):
         a, b = tof(q, -k), tof(q, k)
-        right = net.push(XG.at[c, a], XG.at[c, a], XG.at[c, tof(q, -k - 1)], zdev(1)) if k < 3 or q == 0 else None
-        left = net.push(XG.at[c, b], XG.at[c, b], XG.at[c, tof(q, k + 1)], zdev(7)) if k < 3 or q == 1 else None
-        ring[q, k] = (right, left)
+        right = net.push(part(c, a, h), part(c, a, h), part(c, tof(q, -k - 1), h), zdev(1)) if k < 3 or q == 0 else None
+        left = net.push(part(c, b, h), part(c, b, h), part(c, tof(q, k + 1), h), zdev(7)) if k < 3 or q == 1 else None
+        ring[q, k, h] = (right, left)
 
     def zland(q, k):
-        right, left = ring[q, k]
-        if right is not None:
-            right.wait_recv()
-        if left is not None:
-            left.wait_recv()
-        if k < 3:
-            zsend(q, k + 1)
-        if right is not None:
-            share(k, tof(q, -k - 1))
-        if left is not None:
-            share(k, tof(q, k + 1))
+        for h in range(2):
+            right, left = ring[q, k, h]
+            if right is not None:
+                right.wait_recv()
+            if left is not None:
+                left.wait_recv()
+            if k < 3:
+                zsend(q, k + 1, h)
+            if right is not None:
+                share(k, tof(q, -k - 1), h)
+            if left is not None:
+                share(k, tof(q, k + 1), h)
 
     def normalize(slot):
         wide = XG[0, slot].astype(f32)
@@ -223,15 +227,17 @@
     first.wait_recv()
     for i in range(2):
         XG[i, t] = jnp.concatenate([raw[0, i], raw[1, i]], axis=0).astype(bf)
-    over = net.push(XG.at[c, t], XG.at[c, t], XG.at[c, tof(1, 0)], opp)
-    zsend(0, 0)
+    over = [net.push(part(c, t, h), part(c, t, h), part(c, tof(1, 0), h), opp) for h in range(2)]
+    for h in range(2):
+        zsend(0, 0, h)
     for copy in mine[2:]:
         copy.wait()
     normalize(t)
     yland(0)
-    over.wait_recv()
-    zsend(1, 0)
-    share("y", tof(1, 0))
+    for h in range(2):
+        over[h].wait_recv()
+        zsend(1, 0, h)
+        share("y", tof(1, 0), h)
     zland(0, 0)
     xforward("own", 0, None)
     zland(1, 0)
@@ -306,11 +312,6 @@
     grad_pre = (dact[...] * slope).astype(bf)
     dh[...] = grad_pre
 
-    @pl.loop(0, 8)
-    def _(i):
-        dxp[i] = mm(dh[...], WU[(1 - c) * 8 + i], ((1,), (1,))).astype(bf)
-
-    dx_in = net.push(dxp, dxr, dxr, sib)
     wide_pre = grad_pre.astype(f32)
     dh_t[...] = jnp.transpose(wide_pre).astype(bf)
     act_t[...] = jnp.transpose(0.5 * v * (1.0 + th)).astype(bf)
@@ -353,6 +354,12 @@
                 ysums[u, k] = net.push(Y.at[u, k], YR.at[u, k], YR.at[u, k], ydev(k))
 
     partials(2)
+    @pl.loop(0, 8)
+    def _(i):
+        dxp[i] = mm(dh[...], WU[(1 - c) * 8 + i], ((1,), (1,))).astype(bf)
+
+    dx_in = net.push(dxp, dxr, dxr, sib)
+    partials(1)
     dx_in.wait_recv()
 
     @pl.loop(0, 8)
@@ -370,7 +377,6 @@
     for k in (4, 3, 5, 2, 6, 1, 7):
         for h in range(2):
             zin.append(net.push(dxs.at[h * NZ + (z + k) % NZ], zr.at[k, h], zr.at[k, h], zdev(k)))
-    partials(1)
     pass_on(2)
     partials(3)
     pass_on(1)
@@ -415,8 +421,8 @@
     dn[c] = dn16[pl.ds(pl.multiple_of(c * 8, 8), 8), :]
     for arrival in xg:
         arrival.wait_recv()
-    sums_out[c] = gx[0] + gx[1] + gx[2] + gx[3]
-    last = [net.push(sums_out.at[c], sums_out.at[c], sums_out.at[1 - c], sib)]
+    sums[c] = gx[0] + gx[1] + gx[2] + gx[3]
+    last = [net.push(sums.at[c], sums.at[c], sums.at[1 - c], sib)]
     rows_out.wait_recv()
     d_normed = jnp.concatenate([dn[0], dn[1]], axis=1)
     scaled = d_normed * gain[...]
@@ -445,24 +451,37 @@
     ]
     for copy in mine:
         copy.start()
-    for arrival in last:
+    last[0].wait_recv()
+    for h in range(2):
+        ub_out[:, h * 256 : (h + 1) * 256] = sums[h, 16:17, :]
+        for i in range(8):
+            cols = slice(h * 2048 + i * 256, h * 2048 + (i + 1) * 256)
+            gg_out[:, cols] = sums[h, i : i + 1, :]
+            bg_out[:, cols] = sums[h, 8 + i : 9 + i, :]
+    for arrival in last[1:]:
         arrival.wait_recv()
     for copy in mine:
         copy.wait()
     net.drain()
 
 
+def hand_over(*refs):
+    for source, result in zip(refs[:6], refs[6:]):
+        result[...] = source[...]
+
+
 def shards(tokens, grad_out, norm_gain, norm_bias, up_weight, up_bias, down_weight):
     vmem, hbm = pl.BlockSpec(memory_space=pltpu.VMEM), pl.BlockSpec(memory_space=pltpu.HBM)
     bf, f32 = jnp.bfloat16, jnp.float32
     shape, room = jax.ShapeDtypeStruct, pltpu.VMEM
-    input_grad, up_grad, down_grad, sums = pl.pallas_call(
+    outs = pl.pallas_call(
         kernel,
         out_shape=(
-            shape((8, 4096), bf), shape((128, 512), f32), shape((512, 128), f32), shape((2, 24, 256), f32),
+            shape((8, 4096), bf), shape((128, 512), f32), shape((512, 128), f32),
+            shape((1, 512), f32), shape((1, 4096), f32), shape((1, 4096), f32),
         ),
         in_specs=[vmem, vmem, hbm, hbm, hbm, hbm, hbm],
-        out_specs=(vmem, vmem, vmem, vmem),
+        out_specs=(vmem,) * 6,
         scratch_shapes=[
             room((2, 16, 16, 4096), bf),
             room((16, 16, 4096), bf),
@@ -504,9 +523,10 @@
             room((2, 4, 256, 256), bf),
             room((2, 256, 256), f32),
             room((2, 256, 256), f32),
+            room((2, 24, 256), f32),
             pltpu.SemaphoreType.DMA((5,)),
-            pltpu.SemaphoreType.DMA((180,)),
-            pltpu.SemaphoreType.DMA((180,)),
+            pltpu.SemaphoreType.DMA((220,)),
+            pltpu.SemaphoreType.DMA((220,)),
         ],
         compiler_params=pltpu.CompilerParams(
             collective_id=0, has_side_effects=True, vmem_limit_bytes=63 << 20
@@ -515,9 +535,15 @@
         tokens, grad_out, norm_gain.reshape(1, 4096), norm_bias.reshape(1, 4096),
         up_weight, up_bias.reshape(1, 512), down_weight,
     )
+    outs = pl.pallas_call(
+        hand_over,
+        out_shape=tuple(shape(out.shape, out.dtype) for out in outs),
+        in_specs=[vmem] * 6,
+        out_specs=(vmem,) * 6,
+    )(*outs)
+    input_grad, up_grad, down_grad, up_bias_grad, gain_grad, bias_grad = outs
     return (
-        input_grad, up_grad, down_grad, sums[:, 16].reshape(512),
-        sums[:, 0:8].reshape(4096), sums[:, 8:16].reshape(4096),
+        input_grad, up_grad, down_grad, up_bias_grad.reshape(512), gain_grad.reshape(4096), bias_grad.reshape(4096),
     )
 
 

time: 126 us -> 118 us (0.937)
  local copies, waits for them, and re-layouts: 6.53 us -> 0 us
    unnamed x10 -> x0, local copies, waits for them, and re-layouts: 5.19 us -> none
    pallas_call x1, Pallas kernels: 118 us -> 116 us  [shards(): pl.pallas_call(kernel, out_shape=(shape((8, 4096), bf), shape((128, 512),...]
    pallas_call x0 -> x1, Pallas kernels: none -> 1.91 us  [shards(): pl.pallas_call(hand_over, out_shape=tuple((shape(out.shape, out.dtype) fo...]
    slice x1 -> x0, local copies, waits for them, and re-layouts: 1.34 us -> none  [shards(): sums[:, 16].reshape(512)]
where the time goes in v4:
time: 118 us
  Pallas kernels  118 us (100%)
    pallas_call x1, Pallas kernels, shards(): pl.pallas_call(kernel, out_shape=(shape((8, 4096), bf), shape((128, 512),...  116 us

profile of v4, /device:TPU:25, one launch (start us, length us, event | category | flops | bytes accessed | tf_op | source)
XLA Modules:
  0.0 118.2 jit_solution(2116328794123980976)
XLA Ops:
  0.6 115.6 %shard_map.118 = (bf16[8,4096]{1,0:T(8,128)(2,1)}, f32[128,512]{1,0:T(8,128)}, f32[512,128]{1,0:T(8,128)}, f32[1,512]{1,0:T(1,128)}, f32[1,4096]{1,0:T(1,128)}, /*index=5*/f32[1,4096]{1,0:T(1,128)}) custom-call(bf16[8,4096]{1,0:T(8,128)(2,1)} %tok_in.1, bf16[8,4096]{1,0:T(8,128)(2,1)} %grad_in.1, f32[1,4096]{1,0:T(1,128)} %bitcast.6, f32[1,4096]{1,0:T(1,128)} %bitcast.7, ...), custom_call_target="tpu_custom_call" | custom-call | tf_op jit(solution)/shard_map/pallas_call | solution.py:477
  116.3 1.9 %shard_map.119 = (bf16[8,4096]{1,0:T(8,128)(2,1)}, f32[128,512]{1,0:T(8,128)}, f32[512,128]{1,0:T(8,128)}, f32[1,512]{1,0:T(1,128)}, f32[1,4096]{1,0:T(1,128)}, /*index=5*/f32[1,4096]{1,0:T(1,128)}) custom-call(bf16[8,4096]{1,0:T(8,128)(2,1)} %get-tuple-element.18.refs_0_, f32[128,512]{1,0:T(8,128)} %get-tuple-element.19.refs_1_, ...), custom_call_target="tpu_custom_call" | custom-call | tf_op jit(solution)/shard_map/pallas_call | solution.py:538

commit v5 on v4

v5 whole, which is shorter than its diff:
```python
import functools
import jax
import jax.numpy as jnp
from jax import lax
from jax.experimental import pallas as pl
from jax.experimental.pallas import tpu as pltpu
from jax.sharding import PartitionSpec as P

MESH = pl.DeviceIdType.MESH
NX, NY, NZ = 4, 4, 8


def when(cond, body):
    if cond is None:
        body()
    else:
        pl.when(cond)(body)


class Arrival:
    def __init__(self, copy, cond):
        self.copy, self.cond = copy, cond

    def wait_recv(self):
        when(self.cond, self.copy.wait_recv)

    def wait_send(self):
        when(self.cond, self.copy.wait_send)


class Links:
    def __init__(self, send, recv):
        self.send, self.recv, self.count, self.open = send, recv, 0, []

    def push(self, src, dst, landed, device, go=None, come=None):
        slot = self.count
        self.count += 1
        pair = dict(
            send_sem=self.send.at[slot], recv_sem=self.recv.at[slot], device_id=device, device_id_type=MESH
        )
        when(go, pltpu.make_async_remote_copy(src_ref=src, dst_ref=dst, **pair).start)
        arrival = pltpu.make_async_remote_copy(src_ref=src, dst_ref=landed, **pair)
        self.open.append(Arrival(arrival, go))
        return Arrival(arrival, come)

    def drain(self):
        for arrival in self.open:
            arrival.wait_send()
        self.open = []


def place():
    t, s, c = lax.axis_index("tensor"), lax.axis_index("shard"), lax.axis_index("replica")
    return t, s, c, s // NY, s % NY, t // NZ, t % NZ


def greet(devices):
    barrier = pltpu.get_barrier_semaphore()
    for device in devices:
        pl.semaphore_signal(barrier, inc=1, device_id=device, device_id_type=MESH)
    pl.semaphore_wait(barrier, len(devices))


def mm(left, right, dims):
    return lax.dot_general(left, right, (dims, ((), ())), preferred_element_type=jnp.float32)


def kernel(
    tok_in, grad_in, gain_hbm, nbias_hbm, up_in, ubias_hbm, down_in,
    dx_out, up_out, down_out, ub_out, gg_out, bg_out,
    A, XN, W, gain, nbias, ubias, raw, std, inv, mu, iv, act_t, lt, dh, acc, dacc,
    dxs, zr, zsum, hin, dn16, dn, gz, gh, gsum, gb, gy, gx,
    P, CH, F, CE, DR, Y, YR, keep, ut, sums, local, send, recv,
):
    bf, f32 = jnp.bfloat16, jnp.float32
    t, s, c, x, yl, yh, z = place()
    sib = {"replica": 1 - c}
    xdev = lambda k: {"shard": ((x + k) % NX) * NY + yl}
    ydev = lambda k: {"shard": x * NY + (yl + k) % NY}
    zdev = lambda k: {"tensor": yh * NZ + (z + k) % NZ}
    opp = {"tensor": (1 - yh) * NZ + z}
    sof = lambda dx, dy: ((x + dx + NX) % NX) * NY + (yl + dy + NY) % NY
    tof = lambda dh, dz: ((yh + dh) % 2) * NZ + (z + dz + NZ) % NZ
    net = Links(send, recv)
    first_core, second_core = c == 0, c == 1

    def own_weights(act):
        for core, take in (
            (first_core, lambda h: up_in.at[:, pl.ds(h * 256, 256)]),
            (second_core, lambda h: down_in.at[pl.ds(h * 256, 256), :]),
        ):

            @pl.when(core)
            def _():
                for h in range(2):
                    act(pltpu.make_async_copy(take(h), W.at[s, h], local.at[h]))

    mine = [
        pltpu.make_async_copy(gain_hbm, gain, local.at[2]),
        pltpu.make_async_copy(nbias_hbm, nbias, local.at[3]),
        pltpu.make_async_copy(ubias_hbm, ubias, local.at[4]),
    ]
    own_weights(lambda copy: copy.start())
    for copy in mine:
        copy.start()
    raw[c, 0] = tok_in[...].astype(f32)
    raw[c, 1] = grad_in[...].astype(f32)
    greet([sib, opp] + [xdev(k) for k in (1, 2, 3)] + [ydev(k) for k in (1, 2, 3)] + [zdev(k) for k in range(1, NZ)])
    first = net.push(raw.at[c, 1 - c], raw.at[c, 1 - c], raw.at[1 - c, c], sib)
    own_weights(lambda copy: copy.wait())

    has_left, has_right = yl > 0, yl < NY - 1
    line, xin, far = {}, {}, {}

    def there(side, k):
        return yl - 1 - k >= 0 if side < 0 else yl + 1 + k <= NY - 1

    def along(side, k):
        here, landed = sof(0, side * k), sof(0, side * (k + 1))
        if side < 0:
            go = has_right if k == 0 else jnp.logical_and(has_right, yl - k >= 0)
        else:
            go = has_left if k == 0 else jnp.logical_and(has_left, yl + k <= NY - 1)
        line[side, k] = net.push(W.at[here], W.at[here], W.at[landed], ydev(1 if side < 0 else 3), go, there(side, k))

    def xsend(name, dy, cond):
        here, left, right = sof(0, dy), sof(-1, dy), sof(1, dy)
        xin[name] = [
            net.push(W.at[here, 0], W.at[here, 0], W.at[right, 0], xdev(3), cond, cond),
            net.push(W.at[here, 1], W.at[here, 1], W.at[left, 1], xdev(1), cond, cond),
            net.push(W.at[here, 0], W.at[here, 0], W.at[left, 0], xdev(1), cond, cond),
            net.push(W.at[here, 1], W.at[here, 1], W.at[right, 1], xdev(3), cond, cond),
        ]

    def xforward(name, dy, cond):
        left, right, opposite = sof(-1, dy), sof(1, dy), sof(2, dy)
        xin[name][0].wait_recv()
        one = net.push(W.at[right, 0], W.at[right, 0], W.at[opposite, 0], xdev(3), cond, cond)
        xin[name][1].wait_recv()
        two = net.push(W.at[left, 1], W.at[left, 1], W.at[opposite, 1], xdev(1), cond, cond)
        xin[name][2].wait_recv()
        xin[name][3].wait_recv()
        far[name] = (one, two)

    def yland(k):
        for side in (-1, 1):
            line[side, k].wait_recv()
            if k < 2:
                along(side, k + 1)
            xsend((side, k), side * (k + 1), there(side, k))

    def pass_x(k):
        for side in (-1, 1):
            xforward((side, k), side * (k + 1), there(side, k))

    along(-1, 0)
    along(1, 0)
    xsend("own", 0, None)

    ring = {}

    def part(slot, h):
        return A.at[slot, :, pl.ds(h * 2048, 2048)]

    def zsend(q, k, h):
        a, b = tof(q, -k), tof(q, k)
        right = net.push(part(a, h), part(a, h), part(tof(q, -k - 1), h), zdev(1)) if k < 3 or q == 0 else None
        left = net.push(part(b, h), part(b, h), part(tof(q, k + 1), h), zdev(7)) if k < 3 or q == 1 else None
        ring[q, k, h] = (right, left)

    def zland(q, k):
        for h in range(2):
            for arrival in ring[q, k, h]:
                if arrival is not None:
                    arrival.wait_recv()
            if k < 3:
                zsend(q, k + 1, h)

    def normalize(slot):
        @pl.when(first_core)
        def _():
            wide = A[slot].astype(f32)
            mean = jnp.mean(wide, axis=-1, keepdims=True)
            centred = wide - mean
            istd = lax.rsqrt(jnp.mean(centred * centred, axis=-1, keepdims=True) + 1e-05)
            XN[slot] = (centred * istd * gain[...] + nbias[...]).astype(bf)
            mu[slot] = jnp.broadcast_to(mean, (16, 128))
            iv[slot] = jnp.broadcast_to(istd, (16, 128))

        @pl.when(second_core)
        def _():
            XN[slot] = A[slot]

    def settle(k):
        if k == "y":
            normalize(tof(1, 0))
        elif k < 3:

            @pl.loop(0, 4)
            def _(i):
                normalize(((yh + i // 2) % 2) * NZ + (z + (2 * (i % 2) - 1) * (k + 1) + NZ) % NZ)
        else:

            @pl.loop(0, 2)
            def _(i):
                normalize(((yh + i) % 2) * NZ + (z + 4) % NZ)

    first.wait_recv()
    A[t] = jnp.concatenate([raw[0, c], raw[1, c]], axis=0).astype(bf)
    over = [net.push(part(t, h), part(t, h), part(tof(1, 0), h), opp) for h in range(2)]
    for h in range(2):
        zsend(0, 0, h)
    for copy in mine:
        copy.wait()
    normalize(t)
    yland(0)
    for h in range(2):
        over[h].wait_recv()
        zsend(1, 0, h)
    zland(0, 0)
    xforward("own", 0, None)
    zland(1, 0)
    yland(1)
    settle("y")
    zland(0, 1)
    pass_x(0)
    zland(1, 1)
    yland(2)
    settle(0)
    zland(0, 2)
    zland(1, 2)
    settle(1)
    pass_x(1)
    zland(0, 3)
    zland(1, 3)
    settle(2)
    wide = raw[c, 0]
    centred = wide - jnp.mean(wide, axis=-1, keepdims=True)
    istd = lax.rsqrt(jnp.mean(centred * centred, axis=-1, keepdims=True) + 1e-05)
    inv[...] = jnp.broadcast_to(istd, inv.shape)
    std[...] = centred * istd
    settle(3)

    def forward(s1):
        cols = pl.ds(pl.multiple_of(s1 * 256, 256), 256)
        for core, dims in ((first_core, ((1,), (0,))), (second_core, ((1,), (1,)))):

            @pl.when(core)
            def _():
                right = XN[:, :, cols].reshape(256, 256)
                for h in range(2):
                    acc[h] += mm(right, W[s1, h], dims)

    for h in range(2):
        start = jnp.where(first_core, ubias[:, h * 256 : (h + 1) * 256], 0.0)
        acc[h] = jnp.broadcast_to(start, (256, 256))
    remote = lambda y1: jnp.abs(y1 - yl) == 3
    near = lambda i, y1: ((x + i + i // 2) % NX) * NY + y1

    @pl.loop(0, 12)
    def _(i):
        @pl.when(jnp.logical_not(remote(i // 3)))
        def _():
            forward(near(i % 3, i // 3))

    pass_x(2)
    for name in ("own", (-1, 0), (1, 0), (-1, 1), (1, 1)):
        for arrival in far[name]:
            arrival.wait_recv()

    @pl.loop(0, 4)
    def _(y1):
        @pl.when(jnp.logical_not(remote(y1)))
        def _():
            forward(((x + 2) % NX) * NY + y1)

    ends_line = jnp.logical_or(yl == 0, yl == 3)

    @pl.when(ends_line)
    def _():
        @pl.loop(0, 3)
        def _(i):
            forward(near(i, 3 - yl))

    for name in ((-1, 2), (1, 2)):
        for arrival in far[name]:
            arrival.wait_recv()

    @pl.when(ends_line)
    def _():
        forward(((x + 2) % NX) * NY + 3 - yl)

    d_act_in = net.push(acc, dacc, dacc, sib, second_core, first_core)

    @pl.when(first_core)
    def _():
        root = 0.7978845608028654
        for h in range(2):
            v = acc[h]
            th = jnp.tanh(root * (v + 0.044715 * v * v * v))
            act_t[h] = jnp.transpose(0.5 * v * (1.0 + th)).astype(bf)
            acc[h] = 0.5 * (1.0 + th) + 0.5 * v * (1.0 - th * th) * (root * (1.0 + 3 * 0.044715 * v * v))

    act_in = net.push(act_t, lt, lt, sib, first_core, second_core)
    d_act_in.wait_recv()

    @pl.when(first_core)
    def _():
        gb[32:40, :] = jnp.zeros((8, 256), f32)
        for h in range(2):
            d_pre = (dacc[h] * acc[h]).astype(bf)
            dh[h] = d_pre
            lt[h] = jnp.transpose(d_pre.astype(f32)).astype(bf)
            gb[32 + h : 33 + h, :] = jnp.sum(d_pre.astype(f32), axis=0, keepdims=True)

    act_in.wait_recv()

    chain, direct, ends, ysums = {}, {}, {}, {}

    def partials(k):
        @pl.loop(0, 4)
        def _(i):
            s1 = i * NY + (yl + k) % NY
            cols = pl.ds(pl.multiple_of(s1 * 256, 256), 256)
            right = XN[:, :, cols].reshape(256, 256)
            for h in range(2):
                P[h, s1] = mm(lt[h], right, ((1,), (0,))).astype(bf)

        chain[k] = (
            net.push(P.at[0, sof(2, k)], CH.at[0, k], CH.at[0, k], xdev(3)),
            net.push(P.at[1, sof(2, k)], CH.at[1, k], CH.at[1, k], xdev(1)),
        )
        direct[k] = (
            net.push(P.at[0, sof(1, k)], DR.at[0, k], DR.at[0, k], xdev(1)),
            net.push(P.at[1, sof(-1, k)], DR.at[1, k], DR.at[1, k], xdev(3)),
        )

    def pass_on(k):
        for u, (dx, device) in enumerate(((-1, xdev(3)), (1, xdev(1)))):
            chain[k][u].wait_recv()
            F[u, k] = (CH[u, k].astype(f32) + P[u, sof(dx, k)].astype(f32)).astype(bf)
            ends[u, k] = net.push(F.at[u, k], CE.at[u, k], CE.at[u, k], device)

    def finish_x(k):
        for u in range(2):
            direct[k][u].wait_recv()
            ends[u, k].wait_recv()
            total = P[u, sof(0, k)].astype(f32) + CE[u, k].astype(f32) + DR[u, k].astype(f32)
            if k == 0:
                keep[u] = total
            else:
                Y[u, k] = total.astype(bf)
                ysums[u, k] = net.push(Y.at[u, k], YR.at[u, k], YR.at[u, k], ydev(k))

    def d_normed_part(j):
        @pl.when(first_core)
        def _():
            @pl.loop(0, 8)
            def _(i):
                block = j * 8 + i
                total = mm(dh[0], W[block, 0], ((1,), (1,))) + mm(dh[1], W[block, 1], ((1,), (1,)))
                dxs[j, :, :, pl.ds(pl.multiple_of(i * 256, 256), 256)] = total.astype(bf).reshape(16, 16, 256)
                tok = A[:, :, pl.ds(pl.multiple_of(block * 256, 256), 256)].reshape(256, 256).astype(f32)
                standard = (tok - mu[...].reshape(256, 128)[:, 0:1]) * iv[...].reshape(256, 128)[:, 0:1]
                gsum[pl.ds(block, 1), :] = jnp.sum(total * standard, axis=0, keepdims=True)
                gsum[pl.ds(16 + block, 1), :] = jnp.sum(total, axis=0, keepdims=True)

        for k in (4, 3, 5, 2, 6, 1, 7):
            for h in range(2):
                zin.append(
                    net.push(
                        dxs.at[j, h * NZ + (z + k) % NZ], zr.at[k, h, j], zr.at[k, h, j], zdev(k), first_core, first_core
                    )
                )

    zin = []
    partials(2)
    d_normed_part(0)
    partials(1)
    d_normed_part(1)
    zg = [net.push(gsum, gz.at[k], gz.at[k], zdev(k), first_core, first_core) for k in range(1, NZ)]
    pass_on(2)
    partials(3)
    pass_on(1)
    finish_x(2)
    partials(0)
    for arrival in zg:
        arrival.wait_recv()

    @pl.when(first_core)
    def _():
        total = gsum[...]
        for k in range(1, NZ):
            total += gz[k]
        gb[0:32, :] = total

    hg = net.push(gb.at[0:32, :], gh, gh, opp, first_core, first_core)
    pass_on(3)
    finish_x(1)
    hg.wait_recv()

    @pl.when(first_core)
    def _():
        gy[0, 32:40, :] = gb[32:40, :]
        gy[0, 0:32, :] = gb[0:32, :] + gh[...]

    yg = [net.push(gy.at[0], gy.at[k], gy.at[k], ydev(k), first_core, first_core) for k in (1, 2, 3)]

    for arrival in zin:
        arrival.wait_recv()

    def zadd(h, j):
        total = dxs[j, h * NZ + z].astype(f32)
        for k in range(1, NZ):
            total += zr[k, h, j].astype(f32)
        return total

    @pl.when(first_core)
    def _():
        for j in range(2):
            zsum[j] = zadd(1 - yh, j)

    over = net.push(zsum, hin, hin, opp, first_core, first_core)

    @pl.when(first_core)
    def _():
        for j in range(2):
            dn16[j] = zadd(yh, j)

    pass_on(0)
    finish_x(3)
    for arrival in yg:
        arrival.wait_recv()

    @pl.when(first_core)
    def _():
        gx[0] = gy[0] + gy[1] + gy[2] + gy[3]

    xg = [net.push(gx.at[0], gx.at[k], gx.at[k], xdev(k), first_core, first_core) for k in (1, 2, 3)]
    over.wait_recv()

    @pl.when(first_core)
    def _():
        for j in range(2):
            dn16[j] += hin[j]
            dn[j] = dn16[j, 0:8, :]

    rows_out = net.push(dn16.at[:, 8:16, :], dn, dn, sib, first_core, second_core)
    for arrival in xg:
        arrival.wait_recv()

    @pl.when(first_core)
    def _():
        sums[...] = gx[0] + gx[1] + gx[2] + gx[3]

    last = [net.push(sums, sums, sums, sib, first_core, second_core)]
    rows_out.wait_recv()
    d_normed = jnp.concatenate([dn[0], dn[1]], axis=1)
    scaled = d_normed * gain[...]
    mean1 = jnp.mean(scaled, axis=-1, keepdims=True)
    mean2 = jnp.mean(scaled * std[...], axis=-1, keepdims=True)
    d_in = inv[:, 0:1] * (scaled - mean1 - std[...] * mean2)
    dx_out[...] = (raw[c, 1] + d_in).astype(bf)
    finish_x(0)
    for u in range(2):
        total = keep[u]
        for k in (1, 2, 3):
            ysums[u, k].wait_recv()
            total += YR[u, k].astype(f32)

        @pl.when(first_core)
        def _():
            ut[u] = jnp.transpose(total)

        @pl.when(second_core)
        def _():
            ut[u] = total

    def own_grads(act):
        @pl.when(first_core)
        def _():
            for h in range(2):
                act(pltpu.make_async_copy(ut.at[h, 0:128, :], up_out.at[:, pl.ds(h * 256, 256)], local.at[h]))

        @pl.when(second_core)
        def _():
            for h in range(2):
                act(pltpu.make_async_copy(ut.at[h, :, 128:256], down_out.at[pl.ds(h * 256, 256), :], local.at[h]))

    for h in range(2):
        up_part, down_part = up_out.at[:, pl.ds(h * 256, 256)], down_out.at[pl.ds(h * 256, 256), :]
        last.append(net.push(ut.at[h, 128:256, :], up_part, up_part, sib, first_core, second_core))
        last.append(net.push(ut.at[h, :, 0:128], down_part, down_part, sib, second_core, first_core))
    own_grads(lambda copy: copy.start())
    last[0].wait_recv()
    for h in range(2):
        ub_out[:, h * 256 : (h + 1) * 256] = sums[32 + h : 33 + h, :]
    for i in range(16):
        cols = slice(i * 256, (i + 1) * 256)
        gg_out[:, cols] = sums[i : i + 1, :]
        bg_out[:, cols] = sums[16 + i : 17 + i, :]
    for arrival in last[1:]:
        arrival.wait_recv()
    own_grads(lambda copy: copy.wait())
    net.drain()


def hand_over(*refs):
    for source, result in zip(refs[:6], refs[6:]):
        result[...] = source[...]


def shards(tokens, grad_out, norm_gain, norm_bias, up_weight, up_bias, down_weight):
    vmem, hbm = pl.BlockSpec(memory_space=pltpu.VMEM), pl.BlockSpec(memory_space=pltpu.HBM)
    bf, f32 = jnp.bfloat16, jnp.float32
    shape, room = jax.ShapeDtypeStruct, pltpu.VMEM
    outs = pl.pallas_call(
        kernel,
        out_shape=(
            shape((8, 4096), bf), shape((128, 512), f32), shape((512, 128), f32),
            shape((1, 512), f32), shape((1, 4096), f32), shape((1, 4096), f32),
        ),
        in_specs=[vmem, vmem, hbm, hbm, hbm, hbm, hbm],
        out_specs=(vmem,) * 6,
        scratch_shapes=[
            room((16, 16, 4096), bf),
            room((16, 16, 4096), bf),
            room((16, 2, 256, 256), bf),
            room((1, 4096), f32),
            room((1, 4096), f32),
            room((1, 512), f32),
            room((2, 2, 8, 4096), f32),
            room((8, 4096), f32),
            room((8, 128), f32),
            room((16, 16, 128), f32),
            room((16, 16, 128), f32),
            room((2, 256, 256), bf),
            room((2, 256, 256), bf),
            room((2, 256, 256), bf),
            room((2, 256, 256), f32),
            room((2, 256, 256), f32),
            room((2, 16, 16, 2048), bf),
            room((8, 2, 2, 16, 2048), bf),
            room((2, 16, 2048), f32),
            room((2, 16, 2048), f32),
            room((2, 16, 2048), f32),
            room((2, 8, 2048), f32),
            room((8, 32, 256), f32),
            room((32, 256), f32),
            room((32, 256), f32),
            room((40, 256), f32),
            room((4, 40, 256), f32),
            room((4, 40, 256), f32),
            room((2, 16, 256, 256), bf),
            room((2, 4, 256, 256), bf),
            room((2, 4, 256, 256), bf),
            room((2, 4, 256, 256), bf),
            room((2, 4, 256, 256), bf),
            room((2, 4, 256, 256), bf),
            room((2, 4, 256, 256), bf),
            room((2, 256, 256), f32),
            room((2, 256, 256), f32),
            room((40, 256), f32),
            pltpu.SemaphoreType.DMA((5,)),
            pltpu.SemaphoreType.DMA((220,)),
            pltpu.SemaphoreType.DMA((220,)),
        ],
        compiler_params=pltpu.CompilerParams(
            collective_id=0, has_side_effects=True, vmem_limit_bytes=63 << 20
        ),
    )(
        tokens, grad_out, norm_gain.reshape(1, 4096), norm_bias.reshape(1, 4096),
        up_weight, up_bias.reshape(1, 512), down_weight,
    )
    outs = pl.pallas_call(
        hand_over,
        out_shape=tuple(shape(out.shape, out.dtype) for out in outs),
        in_specs=[vmem] * 6,
        out_specs=(vmem,) * 6,
    )(*outs)
    input_grad, up_grad, down_grad, up_bias_grad, gain_grad, bias_grad = outs
    return (
        input_grad, up_grad, down_grad, up_bias_grad.reshape(512), gain_grad.reshape(4096), bias_grad.reshape(4096),
    )


def solution(mesh):
    return jax.shard_map(
        shards,
        mesh=mesh,
        in_specs=(
            P(("tensor", "shard", "replica"), None),
            P(("tensor", "shard", "replica"), None),
            P(),
            P(),
            P("shard", "tensor"),
            P("tensor"),
            P("tensor", "shard"),
        ),
        out_specs=(
            P(("tensor", "shard", "replica"), None),
            P(("shard", "replica"), "tensor"),
            P("tensor", ("shard", "replica")),
            P("tensor"),
            P(),
            P(),
        ),
        check_vma=False,
    )
```

time: 118 us -> 118 us (level)
  the two profiles are of different devices: /device:TPU:25 before, /device:TPU:1 now
where the time goes in v5:
time: 118 us; the launch traced here: 117 us
  Pallas kernels  117 us (99%)
    pallas_call x1, Pallas kernels, shards(): pl.pallas_call(kernel, out_shape=(shape((8, 4096), bf), shape((128, 512),...  115 us

profile of v5, /device:TPU:1, one launch (start us, length us, event | category | flops | bytes accessed | tf_op | source)
XLA Modules:
  0.0 117.4 jit_solution(9415594803328271767)
XLA Ops:
  0.6 114.8 %shard_map.118 = (bf16[8,4096]{1,0:T(8,128)(2,1)}, f32[128,512]{1,0:T(8,128)}, f32[512,128]{1,0:T(8,128)}, f32[1,512]{1,0:T(1,128)}, f32[1,4096]{1,0:T(1,128)}, /*index=5*/f32[1,4096]{1,0:T(1,128)}) custom-call(bf16[8,4096]{1,0:T(8,128)(2,1)} %tok_in.1, bf16[8,4096]{1,0:T(8,128)(2,1)} %grad_in.1, f32[1,4096]{1,0:T(1,128)} %bitcast.6, f32[1,4096]{1,0:T(1,128)} %bitcast.7, ...), custom_call_target="tpu_custom_call" | custom-call | tf_op jit(solution)/shard_map/pallas_call | solution.py:517
  115.5 1.9 %shard_map.119 = (bf16[8,4096]{1,0:T(8,128)(2,1)}, f32[128,512]{1,0:T(8,128)}, f32[512,128]{1,0:T(8,128)}, f32[1,512]{1,0:T(1,128)}, f32[1,4096]{1,0:T(1,128)}, /*index=5*/f32[1,4096]{1,0:T(1,128)}) custom-call(bf16[8,4096]{1,0:T(8,128)(2,1)} %get-tuple-element.18.refs_0_, f32[128,512]{1,0:T(8,128)} %get-tuple-element.19.refs_1_, ...), custom_call_target="tpu_custom_call" | custom-call | tf_op jit(solution)/shard_map/pallas_call | solution.py:575

commit v6 on v5

--- a/solution.py
+++ b/solution.py
@@ -69,7 +69,7 @@
     tok_in, grad_in, gain_hbm, nbias_hbm, up_in, ubias_hbm, down_in,
     dx_out, up_out, down_out, ub_out, gg_out, bg_out,
     A, XN, W, gain, nbias, ubias, raw, std, inv, mu, iv, act_t, lt, dh, acc, dacc,
-    dxs, zr, zsum, hin, dn16, dn, gz, gh, gsum, gb, gy, gx,
+    dxs, zr, rb, zsum, hin, dn16, dn, gz, gh, gsum, gb, gy, gx,
     P, CH, F, CE, DR, Y, YR, keep, ut, sums, local, send, recv,
 ):
     bf, f32 = jnp.bfloat16, jnp.float32
@@ -365,14 +365,37 @@
                 gsum[pl.ds(block, 1), :] = jnp.sum(total * standard, axis=0, keepdims=True)
                 gsum[pl.ds(16 + block, 1), :] = jnp.sum(total, axis=0, keepdims=True)
 
-        for k in (4, 3, 5, 2, 6, 1, 7):
+        def zpush(to, slot, device, h):
+            return net.push(
+                dxs.at[j, h * NZ + (z + to) % NZ], zr.at[slot, h, j], zr.at[slot, h, j], zdev(device), first_core, first_core
+            )
+
+        joins[j] = [zpush(4, 4, 2, 0), zpush(4, 4, 6, 1)]
+        for h in range(2):
+            joins[j] += [zpush(3, 3, 1, h), zpush(5, 5, 7, h)]
+        for h in range(2):
+            zin.extend([zpush(1, 1, 1, h), zpush(7, 7, 7, h)])
+
+    def join(j):
+        for arrival in joins[j]:
+            arrival.wait_recv()
+
+        @pl.when(first_core)
+        def _():
+            for d, (to, slot) in enumerate(((2, 3), (6, 5))):
+                for h in range(2):
+                    total = dxs[j, h * NZ + (z + to) % NZ].astype(f32) + zr[slot, h, j].astype(f32)
+                    if h == d:
+                        total += zr[4, h, j].astype(f32)
+                    rb[d, h, j] = total.astype(bf)
+
+        for d, to in enumerate((2, 6)):
             for h in range(2):
                 zin.append(
-                    net.push(
-                        dxs.at[j, h * NZ + (z + k) % NZ], zr.at[k, h, j], zr.at[k, h, j], zdev(k), first_core, first_core
-                    )
+                    net.push(rb.at[d, h, j], zr.at[to, h, j], zr.at[to, h, j], zdev(to), first_core, first_core)
                 )
 
+    joins = {}
     zin = []
     partials(2)
     d_normed_part(0)
@@ -380,8 +403,10 @@
     d_normed_part(1)
     zg = [net.push(gsum, gz.at[k], gz.at[k], zdev(k), first_core, first_core) for k in range(1, NZ)]
     pass_on(2)
+    join(0)
     partials(3)
     pass_on(1)
+    join(1)
     finish_x(2)
     partials(0)
     for arrival in zg:
@@ -406,19 +431,20 @@
 
     yg = [net.push(gy.at[0], gy.at[k], gy.at[k], ydev(k), first_core, first_core) for k in (1, 2, 3)]
 
+    pass_on(0)
     for arrival in zin:
         arrival.wait_recv()
 
     def zadd(h, j):
         total = dxs[j, h * NZ + z].astype(f32)
-        for k in range(1, NZ):
+        for k in (1, 7, 2, 6):
             total += zr[k, h, j].astype(f32)
         return total
 
     @pl.when(first_core)
     def _():
         for j in range(2):
-            zsum[j] = zadd(1 - yh, j)
+            zsum[j] = zadd(1 - yh, j).astype(bf)
 
     over = net.push(zsum, hin, hin, opp, first_core, first_core)
 
@@ -427,7 +453,6 @@
         for j in range(2):
             dn16[j] = zadd(yh, j)
 
-    pass_on(0)
     finish_x(3)
     for arrival in yg:
         arrival.wait_recv()
@@ -442,7 +467,7 @@
     @pl.when(first_core)
     def _():
         for j in range(2):
-            dn16[j] += hin[j]
+            dn16[j] += hin[j].astype(f32)
             dn[j] = dn16[j, 0:8, :]
 
     rows_out = net.push(dn16.at[:, 8:16, :], dn, dn, sib, first_core, second_core)
@@ -541,8 +566,9 @@
             room((2, 256, 256), f32),
             room((2, 16, 16, 2048), bf),
             room((8, 2, 2, 16, 2048), bf),
-            room((2, 16, 2048), f32),
-            room((2, 16, 2048), f32),
+            room((2, 2, 2, 16, 2048), bf),
+            room((2, 16, 2048), bf),
+            room((2, 16, 2048), bf),
             room((2, 16, 2048), f32),
             room((2, 8, 2048), f32),
             room((8, 32, 256), f32),

time: 118 us -> 115 us (0.975)
  the two profiles are of different devices: /device:TPU:1 before, /device:TPU:25 now
where the time goes in v6:
time: 115 us; the launch traced here: 114 us
  Pallas kernels  114 us (99%)
    pallas_call x1, Pallas kernels, shards(): pl.pallas_call(kernel, out_shape=(shape((8, 4096), bf), shape((128, 512),...  112 us

profile of v6, /device:TPU:25, one launch (start us, length us, event | category | flops | bytes accessed | tf_op | source)
XLA Modules:
  0.0 114.3 jit_solution(11631222949187502694)
XLA Ops:
  0.6 111.8 %shard_map.118 = (bf16[8,4096]{1,0:T(8,128)(2,1)}, f32[128,512]{1,0:T(8,128)}, f32[512,128]{1,0:T(8,128)}, f32[1,512]{1,0:T(1,128)}, f32[1,4096]{1,0:T(1,128)}, /*index=5*/f32[1,4096]{1,0:T(1,128)}) custom-call(bf16[8,4096]{1,0:T(8,128)(2,1)} %tok_in.1, bf16[8,4096]{1,0:T(8,128)(2,1)} %grad_in.1, f32[1,4096]{1,0:T(1,128)} %bitcast.6, f32[1,4096]{1,0:T(1,128)} %bitcast.7, ...), custom_call_target="tpu_custom_call" | custom-call | tf_op jit(solution)/shard_map/pallas_call | solution.py:542
  112.4 1.9 %shard_map.119 = (bf16[8,4096]{1,0:T(8,128)(2,1)}, f32[128,512]{1,0:T(8,128)}, f32[512,128]{1,0:T(8,128)}, f32[1,512]{1,0:T(1,128)}, f32[1,4096]{1,0:T(1,128)}, /*index=5*/f32[1,4096]{1,0:T(1,128)}) custom-call(bf16[8,4096]{1,0:T(8,128)(2,1)} %get-tuple-element.18.refs_0_, f32[128,512]{1,0:T(8,128)} %get-tuple-element.19.refs_1_, ...), custom_call_target="tpu_custom_call" | custom-call | tf_op jit(solution)/shard_map/pallas_call | solution.py:601

commit v7 on v6

--- a/solution.py
+++ b/solution.py
@@ -126,10 +126,8 @@
     def xsend(name, dy, cond):
         here, left, right = sof(0, dy), sof(-1, dy), sof(1, dy)
         xin[name] = [
-            net.push(W.at[here, 0], W.at[here, 0], W.at[right, 0], xdev(3), cond, cond),
-            net.push(W.at[here, 1], W.at[here, 1], W.at[left, 1], xdev(1), cond, cond),
-            net.push(W.at[here, 0], W.at[here, 0], W.at[left, 0], xdev(1), cond, cond),
-            net.push(W.at[here, 1], W.at[here, 1], W.at[right, 1], xdev(3), cond, cond),
+            net.push(W.at[here], W.at[here], W.at[right], xdev(3), cond, cond),
+            net.push(W.at[here], W.at[here], W.at[left], xdev(1), cond, cond),
         ]
 
     def xforward(name, dy, cond):
@@ -138,8 +136,6 @@
         one = net.push(W.at[right, 0], W.at[right, 0], W.at[opposite, 0], xdev(3), cond, cond)
         xin[name][1].wait_recv()
         two = net.push(W.at[left, 1], W.at[left, 1], W.at[opposite, 1], xdev(1), cond, cond)
-        xin[name][2].wait_recv()
-        xin[name][3].wait_recv()
         far[name] = (one, two)
 
     def yland(k):
@@ -397,10 +393,10 @@
 
     joins = {}
     zin = []
+    d_normed_part(0)
     partials(2)
-    d_normed_part(0)
+    d_normed_part(1)
     partials(1)
-    d_normed_part(1)
     zg = [net.push(gsum, gz.at[k], gz.at[k], zdev(k), first_core, first_core) for k in range(1, NZ)]
     pass_on(2)
     join(0)

time: 115 us -> 114 us (level)
  no operation moved by 1% of the time
where the time goes in v7:
time: 114 us
  Pallas kernels  113 us (99%)
    pallas_call x1, Pallas kernels, shards(): pl.pallas_call(kernel, out_shape=(shape((8, 4096), bf), shape((128, 512),...  111 us

profile of v7, /device:TPU:25, one launch (start us, length us, event | category | flops | bytes accessed | tf_op | source)
XLA Modules:
  0.0 113.9 jit_solution(14125917860218827215)
XLA Ops:
  0.6 111.3 %shard_map.118 = (bf16[8,4096]{1,0:T(8,128)(2,1)}, f32[128,512]{1,0:T(8,128)}, f32[512,128]{1,0:T(8,128)}, f32[1,512]{1,0:T(1,128)}, f32[1,4096]{1,0:T(1,128)}, /*index=5*/f32[1,4096]{1,0:T(1,128)}) custom-call(bf16[8,4096]{1,0:T(8,128)(2,1)} %tok_in.1, bf16[8,4096]{1,0:T(8,128)(2,1)} %grad_in.1, f32[1,4096]{1,0:T(1,128)} %bitcast.6, f32[1,4096]{1,0:T(1,128)} %bitcast.7, ...), custom_call_target="tpu_custom_call" | custom-call | tf_op jit(solution)/shard_map/pallas_call | solution.py:538
  111.9 1.9 %shard_map.119 = (bf16[8,4096]{1,0:T(8,128)(2,1)}, f32[128,512]{1,0:T(8,128)}, f32[512,128]{1,0:T(8,128)}, f32[1,512]{1,0:T(1,128)}, f32[1,4096]{1,0:T(1,128)}, /*index=5*/f32[1,4096]{1,0:T(1,128)}) custom-call(bf16[8,4096]{1,0:T(8,128)(2,1)} %get-tuple-element.18.refs_0_, f32[128,512]{1,0:T(8,128)} %get-tuple-element.19.refs_1_, ...), custom_call_target="tpu_custom_call" | custom-call | tf_op jit(solution)/shard_map/pallas_call | solution.py:597
